TPU v7x, 32 devices: a whole 2x2x4 slice. The times are simulated.
32 devices in a mesh: gx: 4 (over y, x), gy: 8 (over z, core).
Axes of the slice: x: 2, y: 2, z: 4, core: 2. Of those that a mesh axis runs over, the one named last changes fastest.
Arguments:
- permeability: float32 [1, 16, 32, 1024], P(None, None, 'gx', 'gy'), may hold values from 0.2 to 5
- saturation: float32 [1, 16, 32, 1024], P(None, None, 'gx', 'gy'), may hold values from 0.1 to 0.9
- pressure_old: float32 [1, 16, 32, 1024], P(None, None, 'gx', 'gy'), may hold values from -6 to 6
- source: float32 [16, 32, 1024], P(None, 'gx', 'gy'), may hold values from -25 to 25
Outputs:
- pressure: float32 [1, 16, 32, 1024], P(None, None, 'gx', 'gy')
- saturation_new: float32 [1, 16, 32, 1024], P(None, None, 'gx', 'gy')
All inputs are finite; a program needn't handle non-finite values.
Results may differ from a plain program's by a relative error of at most 0.0003.
Values sent between devices are 32-bit elements; how exact they have to be, the bound alone decides.
A program may use at most 64 MiB of HBM per device.

v0:
```python
import jax
import jax.numpy as jnp
from jax import lax
from jax.sharding import PartitionSpec as P

ITERS = 2


storage_term = 0.5
vertical_ratio = 0.1
step_ratio = 0.05
water_viscosity = 1.0
oil_viscosity = 2.0


def padded_2(x, sides, width):
    for axis, dim in sides:
        size, length = (lax.axis_size(axis), x.shape[dim])
        up = [(i, (i + 1) % size) for i in range(size - 1)]
        down = [(j, i) for i, j in up]
        last = lax.slice_in_dim(x, length - width, length, axis=dim)
        first = lax.slice_in_dim(x, 0, width, axis=dim)
        before = lax.ppermute(last, axis, up)
        after = lax.ppermute(first, axis, down)
        x = jnp.concatenate([before, x, after], axis=dim)
    return x


def total_mobility(values):
    return values * values / water_viscosity + (1.0 - values) * (1.0 - values) / oil_viscosity


def water_fraction(values):
    return values * values / water_viscosity / total_mobility(values)


def coefficient(perm_left, perm_right, mobile_left, mobile_right, scaling):
    summed = perm_left + perm_right
    guarded = jnp.where(summed > 0.0, summed, 1.0)
    harmonic = jnp.where(summed > 0.0, 2.0 * perm_left * perm_right / guarded, 0.0)
    return scaling * harmonic * (0.5 * (mobile_left + mobile_right))


def across_pairs(padded, border, margin):
    rows_across = padded.shape[-2] - 2 * border
    rows_along = padded.shape[-1] - 2 * border
    block = padded[
        ...,
        border - margin - 1 : border + rows_across + margin + 1,
        border - margin : border + rows_along + margin,
    ]
    return (block[..., :-1, :], block[..., 1:, :])


def along_pairs(padded, border, margin):
    rows_across = padded.shape[-2] - 2 * border
    rows_along = padded.shape[-1] - 2 * border
    block = padded[
        ...,
        border - margin : border + rows_across + margin,
        border - margin - 1 : border + rows_along + margin + 1,
    ]
    return (block[..., :-1], block[..., 1:])


def interior(padded, border, margin):
    rows_across = padded.shape[-2] - 2 * border
    rows_along = padded.shape[-1] - 2 * border
    return padded[
        ...,
        border - margin : border + rows_across + margin,
        border - margin : border + rows_along + margin,
    ]


def vertical_pairs(values):
    widened = jnp.pad(values, ((0, 0), (1, 1), (0, 0), (0, 0)))
    return (widened[:, :-1], widened[:, 1:])


def face_terms(perm_wide, sat_wide, border, margin):
    mobile = total_mobility(sat_wide)
    perm_left, perm_right = across_pairs(perm_wide, border, margin)
    mobile_left, mobile_right = across_pairs(mobile, border, margin)
    across = coefficient(perm_left, perm_right, mobile_left, mobile_right, 1.0)
    perm_left, perm_right = along_pairs(perm_wide, border, margin)
    mobile_left, mobile_right = along_pairs(mobile, border, margin)
    along = coefficient(perm_left, perm_right, mobile_left, mobile_right, 1.0)
    perm_low, perm_high = vertical_pairs(interior(perm_wide, border, margin))
    mobile_low, mobile_high = vertical_pairs(interior(mobile, border, margin))
    vertical = coefficient(perm_low, perm_high, mobile_low, mobile_high, vertical_ratio)
    return (across, along, vertical)


def divergence(terms):
    across, along, vertical = terms
    return (
        vertical[:, 1:]
        - vertical[:, :-1]
        + (across[..., 1:, :] - across[..., :-1, :])
        + (along[..., 1:] - along[..., :-1])
    )


def diagonal_of(terms):
    across, along, vertical = terms
    return (
        storage_term
        + (vertical[:, 1:] + vertical[:, :-1])
        + (across[..., 1:, :] + across[..., :-1, :])
        + (along[..., 1:] + along[..., :-1])
    )


def fluxes(terms, pressure_wide, border, margin):
    across, along, vertical = terms
    left_side, right_side = across_pairs(pressure_wide, border, margin)
    flow_across = across * (left_side - right_side)
    left_side, right_side = along_pairs(pressure_wide, border, margin)
    flow_along = along * (left_side - right_side)
    lower_side, upper_side = vertical_pairs(interior(pressure_wide, border, margin))
    flow_vertical = vertical * (lower_side - upper_side)
    return (flow_across, flow_along, flow_vertical)


def apply_operator(terms, padded):
    return storage_term * interior(padded, 1, 0) + divergence(fluxes(terms, padded, 1, 0))


def transport(flows, sat_wide, border, margin, inflow_rate):
    fraction = water_fraction(sat_wide)
    flow_across, flow_along, flow_vertical = flows
    left_side, right_side = across_pairs(fraction, border, margin)
    water_across = flow_across * jnp.where(flow_across > 0.0, left_side, right_side)
    left_side, right_side = along_pairs(fraction, border, margin)
    water_along = flow_along * jnp.where(flow_along > 0.0, left_side, right_side)
    middle = interior(fraction, border, margin)
    lower_side, upper_side = vertical_pairs(middle)
    water_vertical = flow_vertical * jnp.where(flow_vertical > 0.0, lower_side, upper_side)
    current = interior(sat_wide, border, margin)
    gained = jnp.maximum(inflow_rate, 0.0) + jnp.minimum(inflow_rate, 0.0) * middle
    return current + step_ratio * (gained - divergence((water_across, water_along, water_vertical)))


def search_image(terms, values):
    padded = padded_2(values, (("gx", 2), ("gy", 3)), 1)
    return (apply_operator(terms, padded), padded)


def local_dot(former, latter):
    return jnp.sum(former * latter, axis=(1, 2, 3))


def per_sample(scalars):
    return scalars[:, None, None, None]


def paired(residual, precond, image_field):
    return lax.psum((local_dot(residual, precond), local_dot(precond, image_field)), ("gx", "gy"))


def local(permeability, saturation, pressure_old, source):
    samples = permeability.shape[0]
    inflow_rate = source[None]
    stacked = jnp.concatenate([permeability, saturation, pressure_old], axis=0)
    padded = padded_2(stacked, (("gx", 2), ("gy", 3)), 1)
    border = 1
    perm_wide = padded[:samples]
    sat_wide = padded[samples : 2 * samples]
    old_wide = padded[2 * samples : 3 * samples]
    wide_terms = face_terms(perm_wide, sat_wide, border, border - 1)
    diagonal = diagonal_of(wide_terms)
    right_side = inflow_rate + storage_term * pressure_old
    solution = pressure_old
    residual = right_side - apply_operator(wide_terms, old_wide)
    precond = residual / diagonal
    image_field, precond_wide = search_image(wide_terms, precond)
    energy_now, curvature = paired(residual, precond, image_field)
    step_size = energy_now / curvature
    direction = precond
    along_image = image_field
    for sweep in range(ITERS):
        solution = solution + per_sample(step_size) * direction
        if sweep + 1 < ITERS:
            residual = residual - per_sample(step_size) * along_image
            precond = residual / diagonal
            image_field, precond_wide = search_image(wide_terms, precond)
            energy_next, curvature = paired(residual, precond, image_field)
            conjugacy = energy_next / energy_now
            step_size = energy_next / (curvature - conjugacy * energy_next / step_size)
            direction = precond + per_sample(conjugacy) * direction
            along_image = image_field + per_sample(conjugacy) * along_image
            energy_now = energy_next
    pressure_wide = padded_2(solution, (("gx", 2), ("gy", 3)), 1)
    flows = fluxes(wide_terms, pressure_wide, 1, 0)
    first = transport(flows, sat_wide, 1, 0, inflow_rate)
    first_wide = padded_2(first, (("gx", 2), ("gy", 3)), 1)
    second = transport(flows, first_wide, 1, 0, inflow_rate)
    return (solution, second)


def solution(mesh):
    in_specs = (
        P(None, None, "gx", "gy"),
        P(None, None, "gx", "gy"),
        P(None, None, "gx", "gy"),
        P(None, "gx", "gy"),
    )
    out_specs = (P(None, None, "gx", "gy"), P(None, None, "gx", "gy"))
    return jax.shard_map(local, mesh=mesh, in_specs=in_specs, out_specs=out_specs, check_vma=False)
```

profile of v0, /device:TPU:1, one launch (start us, length us, event | category | flops | bytes accessed | tf_op | source)
XLA Modules:
  0.0 190.3 jit_solution(136823118898706760)
XLA Ops:
  2.4 3.9 %collective-permute-start = (f32[3,16,1,128]{3,2,1,0:T(1,128)S(1)}, f32[3,16,1,128]{3,2,1,0:T(1,128)S(1)}, u32[]{:S(2)}, u32[]{:S(2)}) collective-permute-start(f32[3,16,1,128]{3,2,1,0:T(1,128)S(1)} %get-tuple-element.26), channel_id=1, source_target_pairs={{0,8},{8,16},{16,24},{1,9},{9,17},{17,25},{2,10},{10,18},{18,26},{... | collective-permute-start | bytes 73736 | tf_op jit(solution)/shard_map/ppermute | solution.py:23
  7.7 3.3 %collective-permute-done.1 = f32[3,16,1,128]{3,2,1,0:T(1,128)S(1)} collective-permute-done((f32[3,16,1,128]{3,2,1,0:T(1,128)S(1)}, f32[3,16,1,128]{3,2,1,0:T(1,128)S(1)}, u32[]{:S(2)}, u32[]{:S(2)}) %collective-permute-start.1) | collective-permute-done | bytes 24608 | tf_op jit(solution)/shard_map/ppermute | solution.py:24
  11.2 5.2 %collective-permute-start.2 = (f32[3,16,10,1]{3,2,1,0:T(8,128)S(1)}, f32[3,16,10,1]{3,2,1,0:T(8,128)S(1)}, u32[]{:S(2)}, u32[]{:S(2)}) collective-permute-start(f32[3,16,10,1]{3,2,1,0:T(8,128)S(1)} %get-tuple-element.24), channel_id=1, source_target_pairs={{0,1},{1,2},{2,3},{3,4},{4,5},{5,6},{6,7},{8,9},{9,10},{10,11},{11... | collective-permute-start | bytes 5768 | tf_op jit(solution)/shard_map/ppermute | solution.py:23
  16.4 1.9 %collective-permute-start.3 = (f32[3,16,10,1]{3,2,1,0:T(8,128)S(1)}, f32[3,16,10,1]{3,2,1,0:T(8,128)S(1)}, u32[]{:S(2)}, u32[]{:S(2)}) collective-permute-start(f32[3,16,10,1]{3,2,1,0:T(8,128)S(1)} %get-tuple-element.25), channel_id=1, source_target_pairs={{1,0},{2,1},{3,2},{4,3},{5,4},{6,5},{7,6},{9,8},{10,9},{11,10},{12... | collective-permute-start | bytes 5768 | tf_op jit(solution)/shard_map/ppermute | solution.py:24
  18.3 2.8 %collective-permute-done.2 = f32[3,16,10,1]{3,2,1,0:T(8,128)S(1)} collective-permute-done((f32[3,16,10,1]{3,2,1,0:T(8,128)S(1)}, f32[3,16,10,1]{3,2,1,0:T(8,128)S(1)}, u32[]{:S(2)}, u32[]{:S(2)}) %collective-permute-start.2) | collective-permute-done | bytes 1952 | tf_op jit(solution)/shard_map/ppermute | solution.py:23
  21.1 4.4 %collective-permute-done.3 = f32[3,16,10,1]{3,2,1,0:T(8,128)S(1)} collective-permute-done((f32[3,16,10,1]{3,2,1,0:T(8,128)S(1)}, f32[3,16,10,1]{3,2,1,0:T(8,128)S(1)}, u32[]{:S(2)}, u32[]{:S(2)}) %collective-permute-start.3) | collective-permute-done | bytes 1952 | tf_op jit(solution)/shard_map/ppermute | solution.py:24
  27.9 4.0 %collective-permute-start.4 = (f32[1,16,1,128]{3,2,1,0:T(1,128)S(1)}, f32[1,16,1,128]{3,2,1,0:T(1,128)S(1)}, u32[]{:S(2)}, u32[]{:S(2)}) collective-permute-start(f32[1,16,1,128]{3,2,1,0:T(1,128)S(1)} %get-tuple-element.42), channel_id=1, source_target_pairs={{0,8},{8,16},{16,24},{1,9},{9,17},{17,25},{2,10},{10,18},{18,26},{... | collective-permute-start | bytes 24584 | tf_op jit(solution)/shard_map/ppermute | solution.py:23
  33.4 3.0 %collective-permute-done.5 = f32[1,16,1,128]{3,2,1,0:T(1,128)S(1)} collective-permute-done((f32[1,16,1,128]{3,2,1,0:T(1,128)S(1)}, f32[1,16,1,128]{3,2,1,0:T(1,128)S(1)}, u32[]{:S(2)}, u32[]{:S(2)}) %collective-permute-start.5) | collective-permute-done | bytes 8224 | tf_op jit(solution)/shard_map/ppermute | solution.py:24
  36.5 3.2 %collective-permute-start.6 = (f32[1,16,10,1]{3,2,1,0:T(8,128)S(1)}, f32[1,16,10,1]{3,2,1,0:T(8,128)S(1)}, u32[]{:S(2)}, u32[]{:S(2)}) collective-permute-start(f32[1,16,10,1]{3,2,1,0:T(8,128)S(1)} %get-tuple-element.34), channel_id=1, source_target_pairs={{0,1},{1,2},{2,3},{3,4},{4,5},{5,6},{6,7},{8,9},{9,10},{10,11},{11... | collective-permute-start | bytes 1928 | tf_op jit(solution)/shard_map/ppermute | solution.py:23
  41.6 4.3 %collective-permute-done.7 = f32[1,16,10,1]{3,2,1,0:T(8,128)S(1)} collective-permute-done((f32[1,16,10,1]{3,2,1,0:T(8,128)S(1)}, f32[1,16,10,1]{3,2,1,0:T(8,128)S(1)}, u32[]{:S(2)}, u32[]{:S(2)}) %collective-permute-start.7) | collective-permute-done | bytes 672 | tf_op jit(solution)/shard_map/ppermute | solution.py:24
  46.8 38.4 %all-reduce.9 = (f32[1]{0:T(128)}, f32[1]{0:T(128)}) all-reduce(f32[1]{0:T(128)} %bitcast.1, f32[1]{0:T(128)} %bitcast.2), channel_id=1, replica_groups=mesh['gx'=4,'gy'=8] {'gx','gy'}, use_global_device_ids=true, to_apply=%region_1.2 | all-reduce | flops 2 | bytes 16 | tf_op jit(solution)/shard_map/psum | solution.py:159
  86.6 3.0 %collective-permute-start.8 = (f32[1,16,1,128]{3,2,1,0:T(1,128)S(1)}, f32[1,16,1,128]{3,2,1,0:T(1,128)S(1)}, u32[]{:S(2)}, u32[]{:S(2)}) collective-permute-start(f32[1,16,1,128]{3,2,1,0:T(1,128)S(1)} %get-tuple-element.40), channel_id=1, source_target_pairs={{0,8},{8,16},{16,24},{1,9},{9,17},{17,25},{2,10},{10,18},{18,26},{... | collective-permute-start | bytes 24584 | tf_op jit(solution)/shard_map/ppermute | solution.py:23
  90.9 3.1 %collective-permute-done.9 = f32[1,16,1,128]{3,2,1,0:T(1,128)S(1)} collective-permute-done((f32[1,16,1,128]{3,2,1,0:T(1,128)S(1)}, f32[1,16,1,128]{3,2,1,0:T(1,128)S(1)}, u32[]{:S(2)}, u32[]{:S(2)}) %collective-permute-start.9) | collective-permute-done | bytes 8224 | tf_op jit(solution)/shard_map/ppermute | solution.py:24
  94.1 5.4 %collective-permute-start.10 = (f32[1,16,10,1]{3,2,1,0:T(8,128)S(1)}, f32[1,16,10,1]{3,2,1,0:T(8,128)S(1)}, u32[]{:S(2)}, u32[]{:S(2)}) collective-permute-start(f32[1,16,10,1]{3,2,1,0:T(8,128)S(1)} %get-tuple-element.32), channel_id=1, source_target_pairs={{0,1},{1,2},{2,3},{3,4},{4,5},{5,6},{6,7},{8,9},{9,10},{10,11},{11... | collective-permute-start | bytes 1928 | tf_op jit(solution)/shard_map/ppermute | solution.py:23
  101.5 4.3 %collective-permute-done.11 = f32[1,16,10,1]{3,2,1,0:T(8,128)S(1)} collective-permute-done((f32[1,16,10,1]{3,2,1,0:T(8,128)S(1)}, f32[1,16,10,1]{3,2,1,0:T(8,128)S(1)}, u32[]{:S(2)}, u32[]{:S(2)}) %collective-permute-start.11) | collective-permute-done | bytes 672 | tf_op jit(solution)/shard_map/ppermute | solution.py:24
  106.8 39.5 %all-reduce.8 = (f32[1]{0:T(128)}, f32[1]{0:T(128)}) all-reduce(f32[1]{0:T(128)} %bitcast.4, f32[1]{0:T(128)} %bitcast.5), channel_id=1, replica_groups=mesh['gx'=4,'gy'=8] {'gx','gy'}, use_global_device_ids=true, to_apply=%region_5.6 | all-reduce | flops 2 | bytes 16 | tf_op jit(solution)/shard_map/psum | solution.py:159
  151.0 2.5 %collective-permute-start.12 = (f32[1,16,1,128]{3,2,1,0:T(1,128)S(1)}, f32[1,16,1,128]{3,2,1,0:T(1,128)S(1)}, u32[]{:S(2)}, u32[]{:S(2)}) collective-permute-start(f32[1,16,1,128]{3,2,1,0:T(1,128)S(1)} %get-tuple-element.38), channel_id=1, source_target_pairs={{0,8},{8,16},{16,24},{1,9},{9,17},{17,25},{2,10},{10,18},{18,26},{... | collective-permute-start | bytes 24584 | tf_op jit(solution)/shard_map/ppermute | solution.py:23
  154.9 3.1 %collective-permute-done.13 = f32[1,16,1,128]{3,2,1,0:T(1,128)S(1)} collective-permute-done((f32[1,16,1,128]{3,2,1,0:T(1,128)S(1)}, f32[1,16,1,128]{3,2,1,0:T(1,128)S(1)}, u32[]{:S(2)}, u32[]{:S(2)}) %collective-permute-start.13) | collective-permute-done | bytes 8224 | tf_op jit(solution)/shard_map/ppermute | solution.py:24
  158.1 5.8 %collective-permute-start.14 = (f32[1,16,10,1]{3,2,1,0:T(8,128)S(1)}, f32[1,16,10,1]{3,2,1,0:T(8,128)S(1)}, u32[]{:S(2)}, u32[]{:S(2)}) collective-permute-start(f32[1,16,10,1]{3,2,1,0:T(8,128)S(1)} %get-tuple-element.30), channel_id=1, source_target_pairs={{0,1},{1,2},{2,3},{3,4},{4,5},{5,6},{6,7},{8,9},{9,10},{10,11},{11... | collective-permute-start | bytes 1928 | tf_op jit(solution)/shard_map/ppermute | solution.py:23
  166.0 4.2 %collective-permute-done.15 = f32[1,16,10,1]{3,2,1,0:T(8,128)S(1)} collective-permute-done((f32[1,16,10,1]{3,2,1,0:T(8,128)S(1)}, f32[1,16,10,1]{3,2,1,0:T(8,128)S(1)}, u32[]{:S(2)}, u32[]{:S(2)}) %collective-permute-start.15) | collective-permute-done | bytes 672 | tf_op jit(solution)/shard_map/ppermute | solution.py:24
  170.5 4.3 %collective-permute-start.16 = (f32[1,16,1,128]{3,2,1,0:T(1,128)S(1)}, f32[1,16,1,128]{3,2,1,0:T(1,128)S(1)}, u32[]{:S(2)}, u32[]{:S(2)}) collective-permute-start(f32[1,16,1,128]{3,2,1,0:T(1,128)S(1)} %get-tuple-element.36), channel_id=1, source_target_pairs={{0,8},{8,16},{16,24},{1,9},{9,17},{17,25},{2,10},{10,18},{18,26},{... | collective-permute-start | bytes 24584 | tf_op jit(solution)/shard_map/ppermute | solution.py:23
  176.1 3.1 %collective-permute-done.17 = f32[1,16,1,128]{3,2,1,0:T(1,128)S(1)} collective-permute-done((f32[1,16,1,128]{3,2,1,0:T(1,128)S(1)}, f32[1,16,1,128]{3,2,1,0:T(1,128)S(1)}, u32[]{:S(2)}, u32[]{:S(2)}) %collective-permute-start.17) | collective-permute-done | bytes 8224 | tf_op jit(solution)/shard_map/ppermute | solution.py:24
  179.3 3.3 %collective-permute-start.18 = (f32[1,16,10,1]{3,2,1,0:T(8,128)S(1)}, f32[1,16,10,1]{3,2,1,0:T(8,128)S(1)}, u32[]{:S(2)}, u32[]{:S(2)}) collective-permute-start(f32[1,16,10,1]{3,2,1,0:T(8,128)S(1)} %get-tuple-element.28), channel_id=1, source_target_pairs={{0,1},{1,2},{2,3},{3,4},{4,5},{5,6},{6,7},{8,9},{9,10},{10,11},{11... | collective-permute-start | bytes 1928 | tf_op jit(solution)/shard_map/ppermute | solution.py:23
  184.6 4.3 %collective-permute-done.19 = f32[1,16,10,1]{3,2,1,0:T(8,128)S(1)} collective-permute-done((f32[1,16,10,1]{3,2,1,0:T(8,128)S(1)}, f32[1,16,10,1]{3,2,1,0:T(8,128)S(1)}, u32[]{:S(2)}, u32[]{:S(2)}) %collective-permute-start.19) | collective-permute-done | bytes 672 | tf_op jit(solution)/shard_map/ppermute | solution.py:24
  (74 shorter events, 22.8 us)
Async XLA Ops:
  0.6 0.9 copy-start.3
  2.4 5.3 %collective-permute-start = (f32[3,16,1,128]{3,2,1,0:T(1,128)S(1)}, f32[3,16,1,128]{3,2,1,0:T(1,128)S(1)}, u32[]{:S(2)}, u32[]{:S(2)}) collective-permute-start(f32[3,16,1,128]{3,2,1,0:T(1,128)S(1)} %get-tuple-element.26), channel_id=1, source_target_pairs={{0,8},{8,16},{16,24},{1,9},{9,17},{17,25},{2,10},{10,18},{18,26},{... | collective-permute-start | bytes 73736 | tf_op jit(solution)/shard_map/ppermute | solution.py:23
  6.4 4.6 %collective-permute-start.1 = (f32[3,16,1,128]{3,2,1,0:T(1,128)S(1)}, f32[3,16,1,128]{3,2,1,0:T(1,128)S(1)}, u32[]{:S(2)}, u32[]{:S(2)}) collective-permute-start(f32[3,16,1,128]{3,2,1,0:T(1,128)S(1)} %get-tuple-element.27), channel_id=1, source_target_pairs={{8,0},{16,8},{24,16},{9,1},{17,9},{25,17},{10,2},{18,10},{26,18},{... | collective-permute-start | bytes 73736 | tf_op jit(solution)/shard_map/ppermute | solution.py:24
  11.2 9.9 %collective-permute-start.2 = (f32[3,16,10,1]{3,2,1,0:T(8,128)S(1)}, f32[3,16,10,1]{3,2,1,0:T(8,128)S(1)}, u32[]{:S(2)}, u32[]{:S(2)}) collective-permute-start(f32[3,16,10,1]{3,2,1,0:T(8,128)S(1)} %get-tuple-element.24), channel_id=1, source_target_pairs={{0,1},{1,2},{2,3},{3,4},{4,5},{5,6},{6,7},{8,9},{9,10},{10,11},{11... | collective-permute-start | bytes 5768 | tf_op jit(solution)/shard_map/ppermute | solution.py:23
  16.4 9.1 %collective-permute-start.3 = (f32[3,16,10,1]{3,2,1,0:T(8,128)S(1)}, f32[3,16,10,1]{3,2,1,0:T(8,128)S(1)}, u32[]{:S(2)}, u32[]{:S(2)}) collective-permute-start(f32[3,16,10,1]{3,2,1,0:T(8,128)S(1)} %get-tuple-element.25), channel_id=1, source_target_pairs={{1,0},{2,1},{3,2},{4,3},{5,4},{6,5},{7,6},{9,8},{10,9},{11,10},{12... | collective-permute-start | bytes 5768 | tf_op jit(solution)/shard_map/ppermute | solution.py:24
  25.8 0.8 copy-start.4
  26.9 0.8 copy-start.2
  27.9 5.4 %collective-permute-start.4 = (f32[1,16,1,128]{3,2,1,0:T(1,128)S(1)}, f32[1,16,1,128]{3,2,1,0:T(1,128)S(1)}, u32[]{:S(2)}, u32[]{:S(2)}) collective-permute-start(f32[1,16,1,128]{3,2,1,0:T(1,128)S(1)} %get-tuple-element.42), channel_id=1, source_target_pairs={{0,8},{8,16},{16,24},{1,9},{9,17},{17,25},{2,10},{10,18},{18,26},{... | collective-permute-start | bytes 24584 | tf_op jit(solution)/shard_map/ppermute | solution.py:23
  31.9 4.4 %collective-permute-start.5 = (f32[1,16,1,128]{3,2,1,0:T(1,128)S(1)}, f32[1,16,1,128]{3,2,1,0:T(1,128)S(1)}, u32[]{:S(2)}, u32[]{:S(2)}) collective-permute-start(f32[1,16,1,128]{3,2,1,0:T(1,128)S(1)} %get-tuple-element.43), channel_id=1, source_target_pairs={{8,0},{16,8},{24,16},{9,1},{17,9},{25,17},{10,2},{18,10},{26,18},{... | collective-permute-start | bytes 24584 | tf_op jit(solution)/shard_map/ppermute | solution.py:24
  36.5 5.2 %collective-permute-start.6 = (f32[1,16,10,1]{3,2,1,0:T(8,128)S(1)}, f32[1,16,10,1]{3,2,1,0:T(8,128)S(1)}, u32[]{:S(2)}, u32[]{:S(2)}) collective-permute-start(f32[1,16,10,1]{3,2,1,0:T(8,128)S(1)} %get-tuple-element.34), channel_id=1, source_target_pairs={{0,1},{1,2},{2,3},{3,4},{4,5},{5,6},{6,7},{8,9},{9,10},{10,11},{11... | collective-permute-start | bytes 1928 | tf_op jit(solution)/shard_map/ppermute | solution.py:23
  39.6 6.3 %collective-permute-start.7 = (f32[1,16,10,1]{3,2,1,0:T(8,128)S(1)}, f32[1,16,10,1]{3,2,1,0:T(8,128)S(1)}, u32[]{:S(2)}, u32[]{:S(2)}) collective-permute-start(f32[1,16,10,1]{3,2,1,0:T(8,128)S(1)} %get-tuple-element.35), channel_id=1, source_target_pairs={{1,0},{2,1},{3,2},{4,3},{5,4},{6,5},{7,6},{9,8},{10,9},{11,10},{12... | collective-permute-start | bytes 1928 | tf_op jit(solution)/shard_map/ppermute | solution.py:24
  86.6 4.4 %collective-permute-start.8 = (f32[1,16,1,128]{3,2,1,0:T(1,128)S(1)}, f32[1,16,1,128]{3,2,1,0:T(1,128)S(1)}, u32[]{:S(2)}, u32[]{:S(2)}) collective-permute-start(f32[1,16,1,128]{3,2,1,0:T(1,128)S(1)} %get-tuple-element.40), channel_id=1, source_target_pairs={{0,8},{8,16},{16,24},{1,9},{9,17},{17,25},{2,10},{10,18},{18,26},{... | collective-permute-start | bytes 24584 | tf_op jit(solution)/shard_map/ppermute | solution.py:23
  89.6 4.4 %collective-permute-start.9 = (f32[1,16,1,128]{3,2,1,0:T(1,128)S(1)}, f32[1,16,1,128]{3,2,1,0:T(1,128)S(1)}, u32[]{:S(2)}, u32[]{:S(2)}) collective-permute-start(f32[1,16,1,128]{3,2,1,0:T(1,128)S(1)} %get-tuple-element.41), channel_id=1, source_target_pairs={{8,0},{16,8},{24,16},{9,1},{17,9},{25,17},{10,2},{18,10},{26,18},{... | collective-permute-start | bytes 24584 | tf_op jit(solution)/shard_map/ppermute | solution.py:24
  94.1 7.4 %collective-permute-start.10 = (f32[1,16,10,1]{3,2,1,0:T(8,128)S(1)}, f32[1,16,10,1]{3,2,1,0:T(8,128)S(1)}, u32[]{:S(2)}, u32[]{:S(2)}) collective-permute-start(f32[1,16,10,1]{3,2,1,0:T(8,128)S(1)} %get-tuple-element.32), channel_id=1, source_target_pairs={{0,1},{1,2},{2,3},{3,4},{4,5},{5,6},{6,7},{8,9},{9,10},{10,11},{11... | collective-permute-start | bytes 1928 | tf_op jit(solution)/shard_map/ppermute | solution.py:23
  99.5 6.3 %collective-permute-start.11 = (f32[1,16,10,1]{3,2,1,0:T(8,128)S(1)}, f32[1,16,10,1]{3,2,1,0:T(8,128)S(1)}, u32[]{:S(2)}, u32[]{:S(2)}) collective-permute-start(f32[1,16,10,1]{3,2,1,0:T(8,128)S(1)} %get-tuple-element.33), channel_id=1, source_target_pairs={{1,0},{2,1},{3,2},{4,3},{5,4},{6,5},{7,6},{9,8},{10,9},{11,10},{12... | collective-permute-start | bytes 1928 | tf_op jit(solution)/shard_map/ppermute | solution.py:24
  151.0 38.4 %copy-start = (f32[1,16,8,128]{3,2,1,0:T(8,128)}, f32[1,16,8,128]{3,2,1,0:T(8,128)S(1)}, u32[]{:S(2)}) copy-start(f32[1,16,8,128]{3,2,1,0:T(8,128)S(1)} %multiply_add_fusion.1) | copy-start | bytes 196612
  151.0 3.9 %collective-permute-start.12 = (f32[1,16,1,128]{3,2,1,0:T(1,128)S(1)}, f32[1,16,1,128]{3,2,1,0:T(1,128)S(1)}, u32[]{:S(2)}, u32[]{:S(2)}) collective-permute-start(f32[1,16,1,128]{3,2,1,0:T(1,128)S(1)} %get-tuple-element.38), channel_id=1, source_target_pairs={{0,8},{8,16},{16,24},{1,9},{9,17},{17,25},{2,10},{10,18},{18,26},{... | collective-permute-start | bytes 24584 | tf_op jit(solution)/shard_map/ppermute | solution.py:23
  153.6 4.4 %collective-permute-start.13 = (f32[1,16,1,128]{3,2,1,0:T(1,128)S(1)}, f32[1,16,1,128]{3,2,1,0:T(1,128)S(1)}, u32[]{:S(2)}, u32[]{:S(2)}) collective-permute-start(f32[1,16,1,128]{3,2,1,0:T(1,128)S(1)} %get-tuple-element.39), channel_id=1, source_target_pairs={{8,0},{16,8},{24,16},{9,1},{17,9},{25,17},{10,2},{18,10},{26,18},{... | collective-permute-start | bytes 24584 | tf_op jit(solution)/shard_map/ppermute | solution.py:24
  158.1 7.9 %collective-permute-start.14 = (f32[1,16,10,1]{3,2,1,0:T(8,128)S(1)}, f32[1,16,10,1]{3,2,1,0:T(8,128)S(1)}, u32[]{:S(2)}, u32[]{:S(2)}) collective-permute-start(f32[1,16,10,1]{3,2,1,0:T(8,128)S(1)} %get-tuple-element.30), channel_id=1, source_target_pairs={{0,1},{1,2},{2,3},{3,4},{4,5},{5,6},{6,7},{8,9},{9,10},{10,11},{11... | collective-permute-start | bytes 1928 | tf_op jit(solution)/shard_map/ppermute | solution.py:23
  163.9 6.3 %collective-permute-start.15 = (f32[1,16,10,1]{3,2,1,0:T(8,128)S(1)}, f32[1,16,10,1]{3,2,1,0:T(8,128)S(1)}, u32[]{:S(2)}, u32[]{:S(2)}) collective-permute-start(f32[1,16,10,1]{3,2,1,0:T(8,128)S(1)} %get-tuple-element.31), channel_id=1, source_target_pairs={{1,0},{2,1},{3,2},{4,3},{5,4},{6,5},{7,6},{9,8},{10,9},{11,10},{12... | collective-permute-start | bytes 1928 | tf_op jit(solution)/shard_map/ppermute | solution.py:24
  170.5 5.6 %collective-permute-start.16 = (f32[1,16,1,128]{3,2,1,0:T(1,128)S(1)}, f32[1,16,1,128]{3,2,1,0:T(1,128)S(1)}, u32[]{:S(2)}, u32[]{:S(2)}) collective-permute-start(f32[1,16,1,128]{3,2,1,0:T(1,128)S(1)} %get-tuple-element.36), channel_id=1, source_target_pairs={{0,8},{8,16},{16,24},{1,9},{9,17},{17,25},{2,10},{10,18},{18,26},{... | collective-permute-start | bytes 24584 | tf_op jit(solution)/shard_map/ppermute | solution.py:23
  174.8 4.4 %collective-permute-start.17 = (f32[1,16,1,128]{3,2,1,0:T(1,128)S(1)}, f32[1,16,1,128]{3,2,1,0:T(1,128)S(1)}, u32[]{:S(2)}, u32[]{:S(2)}) collective-permute-start(f32[1,16,1,128]{3,2,1,0:T(1,128)S(1)} %get-tuple-element.37), channel_id=1, source_target_pairs={{8,0},{16,8},{24,16},{9,1},{17,9},{25,17},{10,2},{18,10},{26,18},{... | collective-permute-start | bytes 24584 | tf_op jit(solution)/shard_map/ppermute | solution.py:24
  179.3 5.2 %collective-permute-start.18 = (f32[1,16,10,1]{3,2,1,0:T(8,128)S(1)}, f32[1,16,10,1]{3,2,1,0:T(8,128)S(1)}, u32[]{:S(2)}, u32[]{:S(2)}) collective-permute-start(f32[1,16,10,1]{3,2,1,0:T(8,128)S(1)} %get-tuple-element.28), channel_id=1, source_target_pairs={{0,1},{1,2},{2,3},{3,4},{4,5},{5,6},{6,7},{8,9},{9,10},{10,11},{11... | collective-permute-start | bytes 1928 | tf_op jit(solution)/shard_map/ppermute | solution.py:23
  182.6 6.3 %collective-permute-start.19 = (f32[1,16,10,1]{3,2,1,0:T(8,128)S(1)}, f32[1,16,10,1]{3,2,1,0:T(8,128)S(1)}, u32[]{:S(2)}, u32[]{:S(2)}) collective-permute-start(f32[1,16,10,1]{3,2,1,0:T(8,128)S(1)} %get-tuple-element.29), channel_id=1, source_target_pairs={{1,0},{2,1},{3,2},{4,3},{5,4},{6,5},{7,6},{9,8},{10,9},{11,10},{12... | collective-permute-start | bytes 1928 | tf_op jit(solution)/shard_map/ppermute | solution.py:24
  (1 other events, 0.8 us)
where the time goes:
time: 191 us; the launch traced here: 190 us
  blocking collectives  77.9 us (41%)
  starting transfers between devices  56.7 us (30%)
  waiting for transfers between devices  39.8 us (21%)
  between operations  7.18 us (4%)
  other arithmetic  4.61 us (2%)
  local copies, waits for them, and re-layouts  4.04 us (2%)
    psum x2, blocking collectives, paired(): lax.psum((local_dot(residual, precond), local_dot(precond, image_field)),...  77.9 us
    ppermute x10, starting transfers between devices, padded_2(): before = lax.ppermute(last, axis, up)  40.7 us
    ppermute x10, waiting for transfers between devices, padded_2(): after = lax.ppermute(first, axis, down)  37 us
    ppermute x10, starting transfers between devices, padded_2(): after = lax.ppermute(first, axis, down)  16.1 us
  transfers between devices with their start and end apart: 20, of which 11 were waited for; matrix products, arithmetic and copies ran while one was open for 0% of the time, Pallas kernels for 0%

commit v1 on v0

v1 whole, which is shorter than its diff:
```python
import functools

import jax
import jax.numpy as jnp
from jax import lax
from jax.experimental import pallas as pl
from jax.experimental.pallas import tpu as pltpu
from jax.sharding import PartitionSpec as P

HALO = 4
STORAGE = 0.5
VERTICAL = 0.1
STEP = 0.05
WATER = 1.0
OIL = 2.0
MESH = pl.DeviceIdType.MESH


def iota(shape, dim):
    return lax.broadcasted_iota(jnp.int32, shape, dim)


class Field:
    def __init__(self, main, side):
        self.main, self.side = main, side

    def map(self, fn, *others):
        return Field(fn(self.main, *[o.main for o in others]), fn(self.side, *[o.side for o in others]))


def fmap(fn, first, *others):
    return first.map(fn, *others)


def row_roll(v, shift):
    axis = v.ndim - 2
    return pltpu.roll(v, shift % v.shape[axis], axis)


def lane_roll(v, shift):
    axis = v.ndim - 1
    shift = shift % v.shape[axis]
    return v if shift == 0 else pltpu.roll(v, shift, axis)


def x_next(f):
    return f.map(lambda v: row_roll(v, -1))


def x_prev(f):
    return f.map(lambda v: row_roll(v, 1))


def z_next(f):
    main = jnp.concatenate([f.main[1:], jnp.zeros_like(f.main[:1])], axis=0)
    width = 2 * HALO
    lanes = f.side.shape[1]
    side = jnp.where(iota(f.side.shape, 1) < lanes - width, lane_roll(f.side, -width), 0.0)
    return Field(main, side)


def z_prev(f):
    main = jnp.concatenate([jnp.zeros_like(f.main[:1]), f.main[:-1]], axis=0)
    width = 2 * HALO
    side = jnp.where(iota(f.side.shape, 1) >= width, lane_roll(f.side, width), 0.0)
    return Field(main, side)


def inserted(side, depth, lane_from, lane_to):
    return jnp.stack([lane_roll(side, lane_to - (2 * HALO * z + lane_from)) for z in range(depth)], axis=0)


def gathered(main, lane_from, lane_to, base):
    width = 2 * HALO
    lane = iota(base.shape, 1)
    for z in range(main.shape[0]):
        base = jnp.where(lane == width * z + lane_to, lane_roll(main[z], width * z + lane_to - lane_from), base)
    return base


def y_next_main(main, side):
    lanes = main.shape[2]
    return jnp.where(
        iota(main.shape, 2) == lanes - 1, inserted(side, main.shape[0], 0, lanes - 1), lane_roll(main, -1)
    )


def y_prev_main(main, side):
    return jnp.where(
        iota(main.shape, 2) == 0, inserted(side, main.shape[0], 2 * HALO - 1, 0), lane_roll(main, 1)
    )


def y_next(f):
    return Field(y_next_main(f.main, f.side), gathered(f.main, 0, 2 * HALO - 1, lane_roll(f.side, -1)))


def y_prev(f):
    return Field(
        y_prev_main(f.main, f.side), gathered(f.main, f.main.shape[2] - 1, 0, lane_roll(f.side, 1))
    )


def mobility(s):
    return s * s / WATER + (1.0 - s) * (1.0 - s) / OIL


def fraction(s):
    water = s * s / WATER
    return water / (water + (1.0 - s) * (1.0 - s) / OIL)


def coefficient(scaling):
    def fn(ka, kb, ma, mb):
        return (scaling * ka * kb / jnp.maximum(ka + kb, 1e-30)) * (ma + mb)

    return fn


NEXT = (z_next, x_next, y_next)
PREV = (z_prev, x_prev, y_prev)


def add(*terms):
    total = terms[0]
    for t in terms[1:]:
        total = total + t
    return total


def packed(own):
    depth, rows, lanes = own.shape
    width = 2 * HALO
    edge = jnp.where(iota(own.shape, 2) < HALO, own, lane_roll(own, width))
    block = iota((rows, lanes), 1) // width
    out = edge[0]
    for z in range(1, depth):
        out = jnp.where(block == z, lane_roll(edge[z], width * z), out)
    return out


def kernel(nx, ny, k_in, s_in, x_in, q_in, p_out, s_out, main_ref, pack_ref, side_ref, part_x, part_y,
           load_sem, xsend, xrecv, psend, precv, rxsend, rxrecv, rysend, ryrecv):
    gx, gy = lax.axis_index("gx"), lax.axis_index("gy")
    ins = (k_in, s_in, x_in, q_in)
    rows = k_in.shape[1]
    wide = rows + 2 * HALO

    def has(dx, dy):
        ok = None
        for d, at, n in ((dx, gx, nx), (dy, gy, ny)):
            if d:
                one = at + d >= 0 if d < 0 else at + d < n
                ok = one if ok is None else ok & one
        return ok

    def at(dx, dy):
        return {"gx": gx + dx, "gy": gy + dy}

    diagonals = [(dx, dy) for dx in (-1, 1) for dy in (-1, 1)]

    loads = [pltpu.make_async_copy(ref, main_ref.at[i, :, pl.ds(0, rows)], load_sem.at[i]) for i, ref in enumerate(ins)]
    for copy in loads:
        copy.start()

    barrier = pltpu.get_barrier_semaphore()
    expected = jnp.int32(nx - 1 + ny - 1)
    for off in range(1, nx):
        pl.semaphore_signal(barrier, inc=1, device_id={"gx": lax.rem(gx + off, nx), "gy": gy}, device_id_type=MESH)
    for off in range(1, ny):
        pl.semaphore_signal(barrier, inc=1, device_id={"gx": gx, "gy": lax.rem(gy + off, ny)}, device_id_type=MESH)
    for dx, dy in diagonals:
        @pl.when(has(dx, dy))
        def _():
            pl.semaphore_signal(barrier, inc=1, device_id=at(dx, dy), device_id_type=MESH)

        expected = expected + has(dx, dy).astype(jnp.int32)

    def edge_rows(dx):
        return pl.ds(0, HALO) if dx < 0 else pl.ds(rows - HALO, HALO)

    def halo_rows(dx):
        return pl.ds(rows, HALO) if dx < 0 else pl.ds(rows + HALO, HALO)

    def x_copies(dx):
        d = (dx + 1) // 2
        return [
            pltpu.make_async_remote_copy(
                src_ref=ref.at[:, edge_rows(dx)],
                dst_ref=main_ref.at[i, :, halo_rows(dx)],
                send_sem=xsend.at[d * len(ins) + i],
                recv_sem=xrecv.at[d * len(ins) + i],
                device_id=at(dx, 0),
                device_id_type=MESH,
            )
            for i, ref in enumerate(ins)
        ]

    def y_copy(dx, dy):
        number = (dx + 1) * 2 + (dy + 1) // 2
        from_rows, to_rows = (edge_rows(dx), halo_rows(dx)) if dx else (pl.ds(0, rows), pl.ds(0, rows))
        return pltpu.make_async_remote_copy(
            src_ref=pack_ref.at[:, from_rows],
            dst_ref=side_ref.at[(1 - dy) // 2, :, to_rows],
            send_sem=psend.at[number],
            recv_sem=precv.at[number],
            device_id=at(dx, dy),
            device_id_type=MESH,
        )

    y_moves = [(0, 1), (0, -1)] + diagonals

    pl.semaphore_wait(barrier, expected)
    for dx in (-1, 1):
        @pl.when(has(dx, 0))
        def _():
            for copy in x_copies(dx):
                copy.start()

    for copy in loads:
        copy.wait()
    for i in range(len(ins)):
        pack_ref[i] = packed(main_ref[i, :, 0:rows, :])
    for dx, dy in y_moves:
        @pl.when(has(dx, dy))
        def _():
            y_copy(dx, dy).start()

    for dx in (-1, 1):
        @pl.when(has(-dx, 0))
        def _():
            for copy in x_copies(dx):
                copy.wait_recv()

    for dx, dy in y_moves:
        @pl.when(has(-dx, -dy))
        def _():
            y_copy(dx, dy).wait_recv()

    lanes = k_in.shape[2]
    depth = k_in.shape[0]
    row = iota((wide, lanes), 0)
    lane = iota((wide, lanes), 1)
    inside = (
        (row < rows)
        | ((row < rows + HALO) & (gx + 1 < nx))
        | ((row >= rows + HALO) & (gx > 0))
    )
    right = lane % (2 * HALO) < HALO
    inside_right = right & inside & (gy + 1 < ny)
    inside_left = jnp.logical_not(right) & inside & (gy > 0)

    def field(i):
        main = jnp.where(inside[None], main_ref[i], 0.0)
        side = jnp.where(inside_right, side_ref[1, i], jnp.where(inside_left, side_ref[0, i], 0.0))
        return Field(main, side)

    k, s, x0, q = (field(i) for i in range(4))
    mob = fmap(mobility, s)
    coefs = []
    for nxt, scaling in zip(NEXT, (VERTICAL, 1.0, 1.0)):
        coefs.append(fmap(coefficient(scaling), k, nxt(k), mob, nxt(mob)))
    before = [prv(c) for prv, c in zip(PREV, coefs)]
    diag = fmap(lambda *c: add(STORAGE, *c), *coefs, *before)
    inverse = fmap(lambda d: 1.0 / d, diag)

    def around(v):
        total = None
        for nxt, prv, c, b in zip(NEXT, PREV, coefs, before):
            term = fmap(lambda c, n, b, p: c * n + b * p, c, nxt(v), b, prv(v))
            total = term if total is None else fmap(jnp.add, total, term)
        return total

    def around_own(v):
        main, side = v.main, v.side[:rows]
        own = main[:, :rows]
        below = jnp.concatenate([own[1:], jnp.zeros_like(own[:1])], axis=0)
        above = jnp.concatenate([jnp.zeros_like(own[:1]), own[:-1]], axis=0)
        moved = (
            (below, above),
            (row_roll(main, -1)[:, :rows], row_roll(main, 1)[:, :rows]),
            (y_next_main(own, side), y_prev_main(own, side)),
        )
        return add(*[c.main[:, :rows] * n + b.main[:, :rows] * p for c, b, (n, p) in zip(coefs, before, moved)])

    r0 = fmap(lambda q, x, d, a: q + STORAGE * x - (d * x - a), q, x0, diag, around(x0))
    u0 = fmap(jnp.multiply, r0, inverse)
    v0 = fmap(lambda d, u, a: d * u - a, diag, u0, around(u0))
    u1 = fmap(jnp.multiply, v0, inverse)
    own_v1 = diag.main[:, :rows] * u1.main[:, :rows] - around_own(u1)

    def own(f):
        return f.main[:, :rows]

    pairs = ((own(r0), own(u0)), (own(u0), own(v0)), (own(v0), own(u1)), (own(u1), own_v1))
    tile_row = iota((rows, lanes), 0)
    part = jnp.zeros((rows, lanes), jnp.float32)
    for i, (left, other) in enumerate(pairs):
        part = jnp.where(tile_row == i, jnp.sum(jnp.sum(left * other, axis=0), axis=0, keepdims=True), part)

    def total_over(value, slots, name, me, n, send, recv):
        def copy(off, slot):
            target = lax.rem(me + off, n)
            return pltpu.make_async_remote_copy(
                src_ref=slots.at[slot], dst_ref=slots.at[slot], send_sem=send.at[off], recv_sem=recv.at[slot],
                device_id={"gx": gx, "gy": gy, name: target}, device_id_type=MESH,
            )

        slots[me] = value
        for off in range(1, n):
            copy(off, me).start()
        for off in range(1, n):
            copy(off, lax.rem(me + off, n)).wait_recv()
        for off in range(1, n):
            copy(off, me).wait_send()
        return add(*[slots[i] for i in range(n)])

    part = total_over(part, part_x, "gx", gx, nx, rxsend, rxrecv)
    part = total_over(part, part_y, "gy", gy, ny, rysend, ryrecv)
    sums = jnp.sum(part, axis=1, keepdims=True)
    sa, sb, sc, sd = (sums[i : i + 1, :] for i in range(4))
    step0 = sa / sb
    next_energy = step0 * step0 * sc - sa
    conjugacy = next_energy / sa
    curvature = sb - 2.0 * step0 * sc + step0 * step0 * sd
    step1 = next_energy / (curvature - conjugacy * next_energy / step0)
    weight0 = step0 + step1 * (1.0 + conjugacy)
    weight1 = -step1 * step0

    pressure = fmap(lambda x, a, b: x + weight0 * a + weight1 * b, x0, u0, u1)
    p_out[...] = own(pressure)
    flows = [fmap(lambda c, a, b: c * (a - b), c, pressure, nxt(pressure)) for nxt, c in zip(NEXT, coefs)]
    inject = fmap(lambda v: jnp.maximum(v, 0.0), q)
    produce = fmap(lambda v: jnp.minimum(v, 0.0), q)

    def transport(current):
        frac = fmap(fraction, current)
        total = fmap(lambda i, o, f: i + o * f, inject, produce, frac)
        for nxt, prv, flow in zip(NEXT, PREV, flows):
            water = fmap(lambda w, a, b: w * jnp.where(w > 0.0, a, b), flow, frac, nxt(frac))
            total = fmap(lambda t, w, p: t - (w - p), total, water, prv(water))
        return fmap(lambda c, t: c + STEP * t, current, total)

    s_out[...] = own(transport(transport(s)))

    for dx in (-1, 1):
        @pl.when(has(dx, 0))
        def _():
            for copy in x_copies(dx):
                copy.wait_send()

    for dx, dy in y_moves:
        @pl.when(has(dx, dy))
        def _():
            y_copy(dx, dy).wait_send()


def local(nx, ny, permeability, saturation, pressure_old, source):
    shape = source.shape
    depth, rows, lanes = shape
    assert permeability.shape[0] == 1 and depth * 2 * HALO == lanes and rows == 2 * HALO
    wide = rows + 2 * HALO
    f32 = jnp.float32
    dma = pltpu.SemaphoreType.DMA
    outs = pl.pallas_call(
        functools.partial(kernel, nx, ny),
        out_shape=[jax.ShapeDtypeStruct(shape, f32)] * 2,
        in_specs=[pl.BlockSpec(memory_space=pl.ANY)] * 4,
        out_specs=[pl.BlockSpec(memory_space=pltpu.VMEM)] * 2,
        scratch_shapes=[
            pltpu.VMEM((4, depth, wide, lanes), f32),
            pltpu.VMEM((4, rows, lanes), f32),
            pltpu.VMEM((2, 4, wide, lanes), f32),
            pltpu.VMEM((nx, rows, lanes), f32),
            pltpu.VMEM((ny, rows, lanes), f32),
            dma((4,)),
            dma((8,)),
            dma((8,)),
            dma((6,)),
            dma((6,)),
            dma((nx,)),
            dma((nx,)),
            dma((ny,)),
            dma((ny,)),
        ],
        compiler_params=pltpu.CompilerParams(
            collective_id=0, has_side_effects=True, vmem_limit_bytes=32 * 1024 * 1024
        ),
    )(permeability[0], saturation[0], pressure_old[0], source)
    return outs[0][None], outs[1][None]


def solution(mesh):
    wide = P(None, None, "gx", "gy")
    return jax.shard_map(
        functools.partial(local, mesh.shape["gx"], mesh.shape["gy"]),
        mesh=mesh,
        in_specs=(wide, wide, wide, P(None, "gx", "gy")),
        out_specs=(wide, wide),
        check_vma=False,
    )
```

time: 191 us -> 27.8 us (0.15)
  the two profiles are of different devices: /device:TPU:1 before, /device:TPU:0 now
where the time goes in v1:
time: 27.8 us; the launch traced here: 27.5 us
  Pallas kernels  22.3 us (80%)
  local copies, waits for them, and re-layouts  4.61 us (17%)
  between operations  0.65 us (2%)
    pallas_call x1, Pallas kernels, local(): pl.pallas_call(functools.partial(kernel, nx, ny), out_shape=[jax.ShapeDty...  22.3 us
    unnamed x10, local copies, waits for them, and re-layouts  4.61 us

profile of v1, /device:TPU:0, one launch (start us, length us, event | category | flops | bytes accessed | tf_op | source)
XLA Modules:
  0.0 27.5 jit_solution(10387346201755624065)
XLA Ops:
  0.6 0.0 copy-start
  0.6 0.8 %copy-done = f32[1,16,8,128]{3,2,1,0:T(8,128)S(1)} copy-done((f32[1,16,8,128]{3,2,1,0:T(8,128)S(1)}, f32[1,16,8,128]{3,2,1,0:T(8,128)}, u32[]{:S(2)}) %copy-start) | copy-done | bytes 65560
  1.5 0.0 copy-start.1
  1.5 0.8 %copy-done.1 = f32[1,16,8,128]{3,2,1,0:T(8,128)S(1)} copy-done((f32[1,16,8,128]{3,2,1,0:T(8,128)S(1)}, f32[1,16,8,128]{3,2,1,0:T(8,128)}, u32[]{:S(2)}) %copy-start.1) | copy-done | bytes 65560
  2.3 0.0 copy-start.2
  2.3 0.8 %copy-done.2 = f32[1,16,8,128]{3,2,1,0:T(8,128)S(1)} copy-done((f32[1,16,8,128]{3,2,1,0:T(8,128)S(1)}, f32[1,16,8,128]{3,2,1,0:T(8,128)}, u32[]{:S(2)}) %copy-start.2) | copy-done | bytes 65560
  3.2 0.0 copy-start.3
  3.2 0.8 %copy-done.3 = f32[16,8,128]{2,1,0:T(8,128)S(1)} copy-done((f32[16,8,128]{2,1,0:T(8,128)S(1)}, f32[16,8,128]{2,1,0:T(8,128)}, u32[]{:S(2)}) %copy-start.3) | copy-done | bytes 65560
  4.0 22.3 %shard_map.59 = (f32[16,8,128]{2,1,0:T(8,128)S(1)}, f32[16,8,128]{2,1,0:T(8,128)S(1)}) custom-call(f32[16,8,128]{2,1,0:T(8,128)S(1)} %bitcast.7, f32[16,8,128]{2,1,0:T(8,128)S(1)} %bitcast.8, f32[16,8,128]{2,1,0:T(8,128)S(1)} %bitcast.9, f32[16,8,128]{2,1,0:T(8,128)S(1)} %copy-done.3), custom_call_target="tpu_custom_call" | custom-call | tf_op jit(solution)/shard_map/pallas_call | solution.py:365
  26.3 0.6 %copy.8 = f32[1,16,8,128]{3,2,1,0:T(8,128)} copy(f32[1,16,8,128]{3,2,1,0:T(8,128)S(1)} %bitcast.6) | data formatting | bytes 131072
  26.9 0.6 %copy.9 = f32[1,16,8,128]{3,2,1,0:T(8,128)} copy(f32[1,16,8,128]{3,2,1,0:T(8,128)S(1)} %bitcast.5) | data formatting | bytes 131072
Async XLA Ops:
  0.6 0.8 %copy-start = (f32[1,16,8,128]{3,2,1,0:T(8,128)S(1)}, f32[1,16,8,128]{3,2,1,0:T(8,128)}, u32[]{:S(2)}) copy-start(f32[1,16,8,128]{3,2,1,0:T(8,128)} %param.4) | copy-start | bytes 196612
  1.5 0.8 %copy-start.1 = (f32[1,16,8,128]{3,2,1,0:T(8,128)S(1)}, f32[1,16,8,128]{3,2,1,0:T(8,128)}, u32[]{:S(2)}) copy-start(f32[1,16,8,128]{3,2,1,0:T(8,128)} %param.5) | copy-start | bytes 196612
  2.3 0.8 %copy-start.2 = (f32[1,16,8,128]{3,2,1,0:T(8,128)S(1)}, f32[1,16,8,128]{3,2,1,0:T(8,128)}, u32[]{:S(2)}) copy-start(f32[1,16,8,128]{3,2,1,0:T(8,128)} %param.6) | copy-start | bytes 196612
  3.2 0.8 %copy-start.3 = (f32[16,8,128]{2,1,0:T(8,128)S(1)}, f32[16,8,128]{2,1,0:T(8,128)}, u32[]{:S(2)}) copy-start(f32[16,8,128]{2,1,0:T(8,128)} %q_in.1) | copy-start | bytes 196612

commit v2 on v1

--- a/solution.py
+++ b/solution.py
@@ -101,18 +101,24 @@
     )
 
 
+def inverted(v):
+    r = pl.reciprocal(v, approx=True)
+    r = r * (2.0 - v * r)
+    return r * (2.0 - v * r)
+
+
 def mobility(s):
     return s * s / WATER + (1.0 - s) * (1.0 - s) / OIL
 
 
 def fraction(s):
     water = s * s / WATER
-    return water / (water + (1.0 - s) * (1.0 - s) / OIL)
+    return water * inverted(water + (1.0 - s) * (1.0 - s) / OIL)
 
 
 def coefficient(scaling):
     def fn(ka, kb, ma, mb):
-        return (scaling * ka * kb / jnp.maximum(ka + kb, 1e-30)) * (ma + mb)
+        return (scaling * ka * kb) * inverted(jnp.maximum(ka + kb, 1e-20)) * (ma + mb)
 
     return fn
 
@@ -262,7 +268,7 @@
         coefs.append(fmap(coefficient(scaling), k, nxt(k), mob, nxt(mob)))
     before = [prv(c) for prv, c in zip(PREV, coefs)]
     diag = fmap(lambda *c: add(STORAGE, *c), *coefs, *before)
-    inverse = fmap(lambda d: 1.0 / d, diag)
+    inverse = fmap(inverted, diag)
 
     def around(v):
         total = None
@@ -365,7 +371,7 @@
     outs = pl.pallas_call(
         functools.partial(kernel, nx, ny),
         out_shape=[jax.ShapeDtypeStruct(shape, f32)] * 2,
-        in_specs=[pl.BlockSpec(memory_space=pl.ANY)] * 4,
+        in_specs=[pl.BlockSpec(memory_space=pltpu.HBM)] * 4,
         out_specs=[pl.BlockSpec(memory_space=pltpu.VMEM)] * 2,
         scratch_shapes=[
             pltpu.VMEM((4, depth, wide, lanes), f32),
@@ -386,7 +392,7 @@
         compiler_params=pltpu.CompilerParams(
             collective_id=0, has_side_effects=True, vmem_limit_bytes=32 * 1024 * 1024
         ),
-    )(permeability[0], saturation[0], pressure_old[0], source)
+    )(*[pltpu.with_memory_space_constraint(v, pltpu.HBM) for v in (permeability[0], saturation[0], pressure_old[0], source)])
     return outs[0][None], outs[1][None]
 
 

time: 27.8 us -> 24.5 us (0.88)
  local copies, waits for them, and re-layouts: 4.61 us -> 1.26 us
    unnamed x10 -> x2, local copies, waits for them, and re-layouts: 4.61 us -> 1.26 us
where the time goes in v2:
time: 24.5 us; the launch traced here: 24.4 us
  Pallas kernels  22.5 us (92%)
  local copies, waits for them, and re-layouts  1.26 us (5%)
  between operations  0.64 us (3%)
    pallas_call x1, Pallas kernels, local(): pl.pallas_call(functools.partial(kernel, nx, ny), out_shape=[jax.ShapeDty...  22.5 us
    unnamed x2, local copies, waits for them, and re-layouts  1.26 us

profile of v2, /device:TPU:0, one launch (start us, length us, event | category | flops | bytes accessed | tf_op | source)
XLA Modules:
  0.0 24.4 jit_solution(1037717441635971790)
XLA Ops:
  0.6 22.5 %shard_map.59 = (f32[16,8,128]{2,1,0:T(8,128)S(1)}, f32[16,8,128]{2,1,0:T(8,128)S(1)}) custom-call(f32[16,8,128]{2,1,0:T(8,128)} %bitcast.7, f32[16,8,128]{2,1,0:T(8,128)} %bitcast.8, f32[16,8,128]{2,1,0:T(8,128)} %bitcast.9, f32[16,8,128]{2,1,0:T(8,128)} %q_in.1), custom_call_target="tpu_custom_call" | custom-call | tf_op jit(solution)/shard_map/pallas_call | solution.py:371
  23.1 0.6 %copy.8 = f32[1,16,8,128]{3,2,1,0:T(8,128)} copy(f32[1,16,8,128]{3,2,1,0:T(8,128)S(1)} %bitcast.6) | data formatting | bytes 131072
  23.7 0.6 %copy.9 = f32[1,16,8,128]{3,2,1,0:T(8,128)} copy(f32[1,16,8,128]{3,2,1,0:T(8,128)S(1)} %bitcast.5) | data formatting | bytes 131072

commit v3 on v2

--- a/solution.py
+++ b/solution.py
@@ -146,7 +146,7 @@
 
 
 def kernel(nx, ny, k_in, s_in, x_in, q_in, p_out, s_out, main_ref, pack_ref, side_ref, part_x, part_y,
-           load_sem, xsend, xrecv, psend, precv, rxsend, rxrecv, rysend, ryrecv):
+           late_send, late_recv, load_sem, xsend, xrecv, psend, precv, rxsend, rxrecv, rysend, ryrecv, lsem, lrecv):
     gx, gy = lax.axis_index("gx"), lax.axis_index("gy")
     ins = (k_in, s_in, x_in, q_in)
     rows = k_in.shape[1]
@@ -182,38 +182,56 @@
 
         expected = expected + has(dx, dy).astype(jnp.int32)
 
-    def edge_rows(dx):
-        return pl.ds(0, HALO) if dx < 0 else pl.ds(rows - HALO, HALO)
-
-    def halo_rows(dx):
-        return pl.ds(rows, HALO) if dx < 0 else pl.ds(rows + HALO, HALO)
-
-    def x_copies(dx):
+    reach = (HALO - 1, HALO - 1, HALO - 1, HALO - 2)
+
+    def edge_rows(dx, width):
+        return pl.ds(0, width) if dx < 0 else pl.ds(rows - width, width)
+
+    def halo_rows(dx, width):
+        return pl.ds(rows, width) if dx < 0 else pl.ds(wide - width, width)
+
+    def x_copies(dx, halves=(0, 1)):
         d = (dx + 1) // 2
         return [
             pltpu.make_async_remote_copy(
-                src_ref=ref.at[:, edge_rows(dx)],
-                dst_ref=main_ref.at[i, :, halo_rows(dx)],
+                src_ref=ref.at[:, edge_rows(dx, reach[i])],
+                dst_ref=main_ref.at[i, :, halo_rows(dx, reach[i])],
                 send_sem=xsend.at[d * len(ins) + i],
                 recv_sem=xrecv.at[d * len(ins) + i],
                 device_id=at(dx, 0),
                 device_id_type=MESH,
             )
             for i, ref in enumerate(ins)
+            if i // 2 in halves
         ]
 
-    def y_copy(dx, dy):
-        number = (dx + 1) * 2 + (dy + 1) // 2
-        from_rows, to_rows = (edge_rows(dx), halo_rows(dx)) if dx else (pl.ds(0, rows), pl.ds(0, rows))
+    def y_copy(half, dx, dy):
+        number = half * 6 + (dx + 1) * 2 + (dy + 1) // 2
+        from_rows = to_rows = pl.ds(0, rows)
+        if dx:
+            from_rows, to_rows = edge_rows(dx, HALO - 1), halo_rows(dx, HALO - 1)
+        arrays = pl.ds(2 * half, 2)
         return pltpu.make_async_remote_copy(
-            src_ref=pack_ref.at[:, from_rows],
-            dst_ref=side_ref.at[(1 - dy) // 2, :, to_rows],
+            src_ref=pack_ref.at[arrays, from_rows],
+            dst_ref=side_ref.at[(1 - dy) // 2, arrays, to_rows],
             send_sem=psend.at[number],
             recv_sem=precv.at[number],
             device_id=at(dx, dy),
             device_id_type=MESH,
         )
 
+    def late_copy(dx):
+        line = pl.ds(1, 1) if dx < 0 else pl.ds(rows - 2, 1)
+        d = (dx + 1) // 2
+        return pltpu.make_async_remote_copy(
+            src_ref=late_send.at[:, line],
+            dst_ref=late_recv.at[:, line],
+            send_sem=lsem.at[d],
+            recv_sem=lrecv.at[d],
+            device_id=at(dx, 0),
+            device_id_type=MESH,
+        )
+
     y_moves = [(0, 1), (0, -1)] + diagonals
 
     pl.semaphore_wait(barrier, expected)
@@ -223,45 +241,47 @@
             for copy in x_copies(dx):
                 copy.start()
 
-    for copy in loads:
-        copy.wait()
-    for i in range(len(ins)):
-        pack_ref[i] = packed(main_ref[i, :, 0:rows, :])
-    for dx, dy in y_moves:
-        @pl.when(has(dx, dy))
-        def _():
-            y_copy(dx, dy).start()
-
-    for dx in (-1, 1):
-        @pl.when(has(-dx, 0))
-        def _():
-            for copy in x_copies(dx):
-                copy.wait_recv()
-
-    for dx, dy in y_moves:
-        @pl.when(has(-dx, -dy))
-        def _():
-            y_copy(dx, dy).wait_recv()
+    for half in range(2):
+        for i in (2 * half, 2 * half + 1):
+            loads[i].wait()
+            pack_ref[i] = packed(main_ref[i, :, 0:rows, :])
+        for dx, dy in y_moves:
+            @pl.when(has(dx, dy))
+            def _():
+                y_copy(half, dx, dy).start()
+
+    def arrive(half):
+        for dx in (-1, 1):
+            @pl.when(has(-dx, 0))
+            def _():
+                for copy in x_copies(dx, (half,)):
+                    copy.wait_recv()
+
+        for dx, dy in y_moves:
+            @pl.when(has(-dx, -dy))
+            def _():
+                y_copy(half, dx, dy).wait_recv()
 
     lanes = k_in.shape[2]
     depth = k_in.shape[0]
     row = iota((wide, lanes), 0)
     lane = iota((wide, lanes), 1)
-    inside = (
-        (row < rows)
-        | ((row < rows + HALO) & (gx + 1 < nx))
-        | ((row >= rows + HALO) & (gx > 0))
-    )
     right = lane % (2 * HALO) < HALO
-    inside_right = right & inside & (gy + 1 < ny)
-    inside_left = jnp.logical_not(right) & inside & (gy > 0)
 
     def field(i):
+        inside = (
+            (row < rows)
+            | ((row < rows + reach[i]) & (gx + 1 < nx))
+            | ((row >= wide - reach[i]) & (gx > 0))
+        )
+        inside_right = right & inside & (gy + 1 < ny)
+        inside_left = jnp.logical_not(right) & inside & (gy > 0)
         main = jnp.where(inside[None], main_ref[i], 0.0)
         side = jnp.where(inside_right, side_ref[1, i], jnp.where(inside_left, side_ref[0, i], 0.0))
         return Field(main, side)
 
-    k, s, x0, q = (field(i) for i in range(4))
+    arrive(0)
+    k, s = field(0), field(1)
     mob = fmap(mobility, s)
     coefs = []
     for nxt, scaling in zip(NEXT, (VERTICAL, 1.0, 1.0)):
@@ -289,6 +309,8 @@
         )
         return add(*[c.main[:, :rows] * n + b.main[:, :rows] * p for c, b, (n, p) in zip(coefs, before, moved)])
 
+    arrive(1)
+    x0, q = field(2), field(3)
     r0 = fmap(lambda q, x, d, a: q + STORAGE * x - (d * x - a), q, x0, diag, around(x0))
     u0 = fmap(jnp.multiply, r0, inverse)
     v0 = fmap(lambda d, u, a: d * u - a, diag, u0, around(u0))
@@ -303,6 +325,8 @@
     part = jnp.zeros((rows, lanes), jnp.float32)
     for i, (left, other) in enumerate(pairs):
         part = jnp.where(tile_row == i, jnp.sum(jnp.sum(left * other, axis=0), axis=0, keepdims=True), part)
+
+    late_send[...] = own(u1)
 
     def total_over(value, slots, name, me, n, send, recv):
         def copy(off, slot):
@@ -312,17 +336,51 @@
                 device_id={"gx": gx, "gy": gy, name: target}, device_id_type=MESH,
             )
 
-        slots[me] = value
-        for off in range(1, n):
-            copy(off, me).start()
-        for off in range(1, n):
-            copy(off, lax.rem(me + off, n)).wait_recv()
-        for off in range(1, n):
-            copy(off, me).wait_send()
-        return add(*[slots[i] for i in range(n)])
-
-    part = total_over(part, part_x, "gx", gx, nx, rxsend, rxrecv)
-    part = total_over(part, part_y, "gy", gy, ny, rysend, ryrecv)
+        def begin():
+            slots[me] = value
+            for off in range(1, n):
+                copy(off, me).start()
+
+        def end():
+            for off in range(1, n):
+                copy(off, lax.rem(me + off, n)).wait_recv()
+            for off in range(1, n):
+                copy(off, me).wait_send()
+            return add(*[slots[i] for i in range(n)])
+
+        return begin, end
+
+    inject = fmap(lambda v: jnp.maximum(v, 0.0), q)
+    produce = fmap(lambda v: jnp.minimum(v, 0.0), q)
+
+    def shares(current):
+        frac = fmap(fraction, current)
+        gained = fmap(lambda i, o, f: i + o * f, inject, produce, frac)
+        return frac, gained, [nxt(frac) for nxt in NEXT]
+
+    begin, end = total_over(part, part_x, "gx", gx, nx, rxsend, rxrecv)
+    begin()
+    for dx in (-1, 1):
+        @pl.when(has(dx, 0))
+        def _():
+            late_copy(dx).start()
+
+    part = end()
+    begin, end = total_over(part, part_y, "gy", gy, ny, rysend, ryrecv)
+    begin()
+    first_shares = shares(s)
+    for dx in (-1, 1):
+        @pl.when(has(-dx, 0))
+        def _():
+            late_copy(dx).wait_recv()
+
+    late = late_recv[...]
+    late_row = iota(late.shape, 1)
+    taken = ((late_row == 1) & (gx + 1 < nx)) | ((late_row == rows - 2) & (gx > 0))
+    u1 = Field(
+        jnp.concatenate([own(u1), jnp.where(taken, late, u1.main[:, rows:])], axis=1), u1.side
+    )
+    part = end()
     sums = jnp.sum(part, axis=1, keepdims=True)
     sa, sb, sc, sd = (sums[i : i + 1, :] for i in range(4))
     step0 = sa / sb
@@ -336,29 +394,28 @@
     pressure = fmap(lambda x, a, b: x + weight0 * a + weight1 * b, x0, u0, u1)
     p_out[...] = own(pressure)
     flows = [fmap(lambda c, a, b: c * (a - b), c, pressure, nxt(pressure)) for nxt, c in zip(NEXT, coefs)]
-    inject = fmap(lambda v: jnp.maximum(v, 0.0), q)
-    produce = fmap(lambda v: jnp.minimum(v, 0.0), q)
-
-    def transport(current):
-        frac = fmap(fraction, current)
-        total = fmap(lambda i, o, f: i + o * f, inject, produce, frac)
-        for nxt, prv, flow in zip(NEXT, PREV, flows):
-            water = fmap(lambda w, a, b: w * jnp.where(w > 0.0, a, b), flow, frac, nxt(frac))
+    def transport(current, share):
+        frac, total, after = share
+        for prv, flow, nf in zip(PREV, flows, after):
+            water = fmap(lambda w, a, b: w * jnp.where(w > 0.0, a, b), flow, frac, nf)
             total = fmap(lambda t, w, p: t - (w - p), total, water, prv(water))
         return fmap(lambda c, t: c + STEP * t, current, total)
 
-    s_out[...] = own(transport(transport(s)))
+    first = transport(s, first_shares)
+    s_out[...] = own(transport(first, shares(first)))
 
     for dx in (-1, 1):
         @pl.when(has(dx, 0))
         def _():
             for copy in x_copies(dx):
                 copy.wait_send()
+            late_copy(dx).wait_send()
 
     for dx, dy in y_moves:
         @pl.when(has(dx, dy))
         def _():
-            y_copy(dx, dy).wait_send()
+            for half in range(2):
+                y_copy(half, dx, dy).wait_send()
 
 
 def local(nx, ny, permeability, saturation, pressure_old, source):
@@ -379,15 +436,19 @@
             pltpu.VMEM((2, 4, wide, lanes), f32),
             pltpu.VMEM((nx, rows, lanes), f32),
             pltpu.VMEM((ny, rows, lanes), f32),
+            pltpu.VMEM(shape, f32),
+            pltpu.VMEM(shape, f32),
             dma((4,)),
             dma((8,)),
             dma((8,)),
-            dma((6,)),
-            dma((6,)),
+            dma((12,)),
+            dma((12,)),
             dma((nx,)),
             dma((nx,)),
             dma((ny,)),
             dma((ny,)),
+            dma((2,)),
+            dma((2,)),
         ],
         compiler_params=pltpu.CompilerParams(
             collective_id=0, has_side_effects=True, vmem_limit_bytes=32 * 1024 * 1024

time: 24.5 us -> 22.6 us (0.922)
  Pallas kernels: 22.5 us -> 20.6 us
    pallas_call x1, Pallas kernels: 22.5 us -> 20.6 us  [local(): pl.pallas_call(functools.partial(kernel, nx, ny), out_shape=[jax.ShapeDty...]
where the time goes in v3:
time: 22.6 us; the launch traced here: 22.5 us
  Pallas kernels  20.6 us (91%)
  local copies, waits for them, and re-layouts  1.26 us (6%)
  between operations  0.64 us (3%)
    pallas_call x1, Pallas kernels, local(): pl.pallas_call(functools.partial(kernel, nx, ny), out_shape=[jax.ShapeDty...  20.6 us
    unnamed x2, local copies, waits for them, and re-layouts  1.26 us

profile of v3, /device:TPU:0, one launch (start us, length us, event | category | flops | bytes accessed | tf_op | source)
XLA Modules:
  0.0 22.5 jit_solution(9786659925438030376)
XLA Ops:
  0.6 20.6 %shard_map.59 = (f32[16,8,128]{2,1,0:T(8,128)S(1)}, f32[16,8,128]{2,1,0:T(8,128)S(1)}) custom-call(f32[16,8,128]{2,1,0:T(8,128)} %bitcast.7, f32[16,8,128]{2,1,0:T(8,128)} %bitcast.8, f32[16,8,128]{2,1,0:T(8,128)} %bitcast.9, f32[16,8,128]{2,1,0:T(8,128)} %q_in.1), custom_call_target="tpu_custom_call" | custom-call | tf_op jit(solution)/shard_map/pallas_call | solution.py:428
  21.2 0.6 %copy.8 = f32[1,16,8,128]{3,2,1,0:T(8,128)} copy(f32[1,16,8,128]{3,2,1,0:T(8,128)S(1)} %bitcast.6) | data formatting | bytes 131072
  21.9 0.6 %copy.9 = f32[1,16,8,128]{3,2,1,0:T(8,128)} copy(f32[1,16,8,128]{3,2,1,0:T(8,128)S(1)} %bitcast.5) | data formatting | bytes 131072

commit v4 on v3

--- a/solution.py
+++ b/solution.py
@@ -145,8 +145,8 @@
     return out
 
 
-def kernel(nx, ny, k_in, s_in, x_in, q_in, p_out, s_out, main_ref, pack_ref, side_ref, part_x, part_y,
-           late_send, late_recv, load_sem, xsend, xrecv, psend, precv, rxsend, rxrecv, rysend, ryrecv, lsem, lrecv):
+def kernel(nx, ny, k_in, s_in, x_in, q_in, p_out, s_out, main_ref, pack_ref, side_ref, slots,
+           late_send, late_recv, load_sem, xsend, xrecv, psend, precv, rsend, rrecv, ready, lsem, lrecv):
     gx, gy = lax.axis_index("gx"), lax.axis_index("gy")
     ins = (k_in, s_in, x_in, q_in)
     rows = k_in.shape[1]
@@ -241,6 +241,9 @@
             for copy in x_copies(dx):
                 copy.start()
 
+    for off in range(1, nx):
+        pl.semaphore_signal(ready, inc=1, device_id={"gx": lax.rem(gx + off, nx), "gy": gy}, device_id_type=MESH)
+
     for half in range(2):
         for i in (2 * half, 2 * half + 1):
             loads[i].wait()
@@ -328,27 +331,28 @@
 
     late_send[...] = own(u1)
 
-    def total_over(value, slots, name, me, n, send, recv):
-        def copy(off, slot):
-            target = lax.rem(me + off, n)
-            return pltpu.make_async_remote_copy(
-                src_ref=slots.at[slot], dst_ref=slots.at[slot], send_sem=send.at[off], recv_sem=recv.at[slot],
-                device_id={"gx": gx, "gy": gy, name: target}, device_id_type=MESH,
-            )
-
-        def begin():
-            slots[me] = value
-            for off in range(1, n):
-                copy(off, me).start()
-
-        def end():
-            for off in range(1, n):
-                copy(off, lax.rem(me + off, n)).wait_recv()
-            for off in range(1, n):
-                copy(off, me).wait_send()
-            return add(*[slots[i] for i in range(n)])
-
-        return begin, end
+    count = nx * ny
+    group = lanes // 4
+    folded = part + lane_roll(part, lanes // 2)
+    folded = folded + lane_roll(folded, lanes // 4)
+    mine = iota((rows, lanes), 1) // group == iota((rows, lanes), 0)
+    slots[0:1, :] = jnp.sum(jnp.where(mine, folded, 0.0), axis=0, keepdims=True)
+    me = gx * ny + gy
+
+    def share_copy(off, first, size):
+        target = lax.rem(me + off, count)
+        return pltpu.make_async_remote_copy(
+            src_ref=slots.at[pl.ds(0 if size == 1 else first, size)],
+            dst_ref=slots.at[pl.ds(first, size)],
+            send_sem=rsend,
+            recv_sem=rrecv,
+            device_id={"gx": target // ny, "gy": target % ny},
+            device_id_type=MESH,
+        )
+
+    pl.semaphore_wait(ready, nx - 1)
+    for off in range(1, count):
+        share_copy(off, off, 1).start()
 
     inject = fmap(lambda v: jnp.maximum(v, 0.0), q)
     produce = fmap(lambda v: jnp.minimum(v, 0.0), q)
@@ -358,16 +362,11 @@
         gained = fmap(lambda i, o, f: i + o * f, inject, produce, frac)
         return frac, gained, [nxt(frac) for nxt in NEXT]
 
-    begin, end = total_over(part, part_x, "gx", gx, nx, rxsend, rxrecv)
-    begin()
     for dx in (-1, 1):
         @pl.when(has(dx, 0))
         def _():
             late_copy(dx).start()
 
-    part = end()
-    begin, end = total_over(part, part_y, "gy", gy, ny, rysend, ryrecv)
-    begin()
     first_shares = shares(s)
     for dx in (-1, 1):
         @pl.when(has(-dx, 0))
@@ -380,8 +379,9 @@
     u1 = Field(
         jnp.concatenate([own(u1), jnp.where(taken, late, u1.main[:, rows:])], axis=1), u1.side
     )
-    part = end()
-    sums = jnp.sum(part, axis=1, keepdims=True)
+    share_copy(1, 1, count - 1).wait_recv()
+    total = jnp.sum(slots[...], axis=0, keepdims=True)
+    sums = jnp.sum(jnp.where(mine, total, 0.0), axis=1, keepdims=True)
     sa, sb, sc, sd = (sums[i : i + 1, :] for i in range(4))
     step0 = sa / sb
     next_energy = step0 * step0 * sc - sa
@@ -416,6 +416,8 @@
         def _():
             for half in range(2):
                 y_copy(half, dx, dy).wait_send()
+
+    share_copy(1, 1, count - 1).wait_send()
 
 
 def local(nx, ny, permeability, saturation, pressure_old, source):
@@ -434,8 +436,7 @@
             pltpu.VMEM((4, depth, wide, lanes), f32),
             pltpu.VMEM((4, rows, lanes), f32),
             pltpu.VMEM((2, 4, wide, lanes), f32),
-            pltpu.VMEM((nx, rows, lanes), f32),
-            pltpu.VMEM((ny, rows, lanes), f32),
+            pltpu.VMEM((nx * ny, lanes), f32),
             pltpu.VMEM(shape, f32),
             pltpu.VMEM(shape, f32),
             dma((4,)),
@@ -443,10 +444,9 @@
             dma((8,)),
             dma((12,)),
             dma((12,)),
-            dma((nx,)),
-            dma((nx,)),
-            dma((ny,)),
-            dma((ny,)),
+            dma,
+            dma,
+            pltpu.SemaphoreType.REGULAR,
             dma((2,)),
             dma((2,)),
         ],

time: 22.6 us -> 20.4 us (0.903)
  Pallas kernels: 20.6 us -> 18.4 us
    pallas_call x1, Pallas kernels: 20.6 us -> 18.4 us  [local(): pl.pallas_call(functools.partial(kernel, nx, ny), out_shape=[jax.ShapeDty...]
where the time goes in v4:
time: 20.4 us; the launch traced here: 20.3 us
  Pallas kernels  18.4 us (90%)
  local copies, waits for them, and re-layouts  1.26 us (6%)
  between operations  0.64 us (3%)
    pallas_call x1, Pallas kernels, local(): pl.pallas_call(functools.partial(kernel, nx, ny), out_shape=[jax.ShapeDty...  18.4 us
    unnamed x2, local copies, waits for them, and re-layouts  1.26 us

profile of v4, /device:TPU:0, one launch (start us, length us, event | category | flops | bytes accessed | tf_op | source)
XLA Modules:
  0.0 20.3 jit_solution(4360981586018774265)
XLA Ops:
  0.6 18.4 %shard_map.59 = (f32[16,8,128]{2,1,0:T(8,128)S(1)}, f32[16,8,128]{2,1,0:T(8,128)S(1)}) custom-call(f32[16,8,128]{2,1,0:T(8,128)} %bitcast.7, f32[16,8,128]{2,1,0:T(8,128)} %bitcast.8, f32[16,8,128]{2,1,0:T(8,128)} %bitcast.9, f32[16,8,128]{2,1,0:T(8,128)} %q_in.1), custom_call_target="tpu_custom_call" | custom-call | tf_op jit(solution)/shard_map/pallas_call | solution.py:430
  19.0 0.6 %copy.8 = f32[1,16,8,128]{3,2,1,0:T(8,128)} copy(f32[1,16,8,128]{3,2,1,0:T(8,128)S(1)} %bitcast.6) | data formatting | bytes 131072
  19.6 0.6 %copy.9 = f32[1,16,8,128]{3,2,1,0:T(8,128)} copy(f32[1,16,8,128]{3,2,1,0:T(8,128)S(1)} %bitcast.5) | data formatting | bytes 131072

commit v5 on v4

--- a/solution.py
+++ b/solution.py
@@ -8,6 +8,7 @@
 from jax.sharding import PartitionSpec as P
 
 HALO = 4
+BLOCK = 4
 STORAGE = 0.5
 VERTICAL = 0.1
 STEP = 0.05
@@ -21,15 +22,11 @@
 
 
 class Field:
-    def __init__(self, main, side):
-        self.main, self.side = main, side
-
-    def map(self, fn, *others):
-        return Field(fn(self.main, *[o.main for o in others]), fn(self.side, *[o.side for o in others]))
-
-
-def fmap(fn, first, *others):
-    return first.map(fn, *others)
+    def __init__(self, blocks, side):
+        self.blocks, self.side = blocks, side
+
+    def at(self, i):
+        return self.side if i is None else self.blocks[i]
 
 
 def row_roll(v, shift):
@@ -43,62 +40,61 @@
     return v if shift == 0 else pltpu.roll(v, shift, axis)
 
 
-def x_next(f):
-    return f.map(lambda v: row_roll(v, -1))
-
-
-def x_prev(f):
-    return f.map(lambda v: row_roll(v, 1))
-
-
-def z_next(f):
-    main = jnp.concatenate([f.main[1:], jnp.zeros_like(f.main[:1])], axis=0)
+def x_next(f, i):
+    return row_roll(f.at(i), -1)
+
+
+def x_prev(f, i):
+    return row_roll(f.at(i), 1)
+
+
+def z_next(f, i):
     width = 2 * HALO
-    lanes = f.side.shape[1]
-    side = jnp.where(iota(f.side.shape, 1) < lanes - width, lane_roll(f.side, -width), 0.0)
-    return Field(main, side)
-
-
-def z_prev(f):
-    main = jnp.concatenate([jnp.zeros_like(f.main[:1]), f.main[:-1]], axis=0)
+    if i is None:
+        lanes = f.side.shape[1]
+        return jnp.where(iota(f.side.shape, 1) < lanes - width, lane_roll(f.side, -width), 0.0)
+    b = f.blocks[i]
+    last = f.blocks[i + 1][:1] if i + 1 < len(f.blocks) else jnp.zeros_like(b[:1])
+    return jnp.concatenate([b[1:], last], axis=0)
+
+
+def z_prev(f, i):
     width = 2 * HALO
-    side = jnp.where(iota(f.side.shape, 1) >= width, lane_roll(f.side, width), 0.0)
-    return Field(main, side)
-
-
-def inserted(side, depth, lane_from, lane_to):
-    return jnp.stack([lane_roll(side, lane_to - (2 * HALO * z + lane_from)) for z in range(depth)], axis=0)
-
-
-def gathered(main, lane_from, lane_to, base):
+    if i is None:
+        return jnp.where(iota(f.side.shape, 1) >= width, lane_roll(f.side, width), 0.0)
+    b = f.blocks[i]
+    first = f.blocks[i - 1][-1:] if i else jnp.zeros_like(b[:1])
+    return jnp.concatenate([first, b[:-1]], axis=0)
+
+
+def inserted(side, i, lane_from, lane_to):
+    planes = range(i * BLOCK, (i + 1) * BLOCK)
+    return jnp.stack([lane_roll(side, lane_to - (2 * HALO * z + lane_from)) for z in planes], axis=0)
+
+
+def gathered(blocks, lane_from, lane_to, base):
     width = 2 * HALO
     lane = iota(base.shape, 1)
-    for z in range(main.shape[0]):
-        base = jnp.where(lane == width * z + lane_to, lane_roll(main[z], width * z + lane_to - lane_from), base)
+    for i, b in enumerate(blocks):
+        for j in range(BLOCK):
+            to = width * (i * BLOCK + j) + lane_to
+            base = jnp.where(lane == to, lane_roll(b[j], to - lane_from), base)
     return base
 
 
-def y_next_main(main, side):
-    lanes = main.shape[2]
-    return jnp.where(
-        iota(main.shape, 2) == lanes - 1, inserted(side, main.shape[0], 0, lanes - 1), lane_roll(main, -1)
-    )
-
-
-def y_prev_main(main, side):
-    return jnp.where(
-        iota(main.shape, 2) == 0, inserted(side, main.shape[0], 2 * HALO - 1, 0), lane_roll(main, 1)
-    )
-
-
-def y_next(f):
-    return Field(y_next_main(f.main, f.side), gathered(f.main, 0, 2 * HALO - 1, lane_roll(f.side, -1)))
-
-
-def y_prev(f):
-    return Field(
-        y_prev_main(f.main, f.side), gathered(f.main, f.main.shape[2] - 1, 0, lane_roll(f.side, 1))
-    )
+def y_next(f, i):
+    if i is None:
+        return gathered(f.blocks, 0, 2 * HALO - 1, lane_roll(f.side, -1))
+    b = f.blocks[i]
+    lanes = b.shape[2]
+    return jnp.where(iota(b.shape, 2) == lanes - 1, inserted(f.side, i, 0, lanes - 1), lane_roll(b, -1))
+
+
+def y_prev(f, i):
+    if i is None:
+        return gathered(f.blocks, f.blocks[0].shape[2] - 1, 0, lane_roll(f.side, 1))
+    b = f.blocks[i]
+    return jnp.where(iota(b.shape, 2) == 0, inserted(f.side, i, 2 * HALO - 1, 0), lane_roll(b, 1))
 
 
 def inverted(v):
@@ -125,6 +121,12 @@
 
 NEXT = (z_next, x_next, y_next)
 PREV = (z_prev, x_prev, y_prev)
+
+
+def build(fn, count):
+    side = fn(None)
+    blocks = [fn(i) for i in range(count)]
+    return [Field([b[n] for b in blocks], side[n]) for n in range(len(side))]
 
 
 def add(*terms):
@@ -271,6 +273,8 @@
     lane = iota((wide, lanes), 1)
     right = lane % (2 * HALO) < HALO
 
+    nb = depth // BLOCK
+
     def field(i):
         inside = (
             (row < rows)
@@ -279,55 +283,68 @@
         )
         inside_right = right & inside & (gy + 1 < ny)
         inside_left = jnp.logical_not(right) & inside & (gy > 0)
-        main = jnp.where(inside[None], main_ref[i], 0.0)
+        blocks = [jnp.where(inside[None], main_ref[i, n * BLOCK : (n + 1) * BLOCK], 0.0) for n in range(nb)]
         side = jnp.where(inside_right, side_ref[1, i], jnp.where(inside_left, side_ref[0, i], 0.0))
-        return Field(main, side)
+        return Field(blocks, side)
+
+    def own(f):
+        return jnp.concatenate([b[:, :rows] for b in f.blocks], axis=0)
 
     arrive(0)
     k, s = field(0), field(1)
-    mob = fmap(mobility, s)
-    coefs = []
-    for nxt, scaling in zip(NEXT, (VERTICAL, 1.0, 1.0)):
-        coefs.append(fmap(coefficient(scaling), k, nxt(k), mob, nxt(mob)))
-    before = [prv(c) for prv, c in zip(PREV, coefs)]
-    diag = fmap(lambda *c: add(STORAGE, *c), *coefs, *before)
-    inverse = fmap(inverted, diag)
-
-    def around(v):
-        total = None
-        for nxt, prv, c, b in zip(NEXT, PREV, coefs, before):
-            term = fmap(lambda c, n, b, p: c * n + b * p, c, nxt(v), b, prv(v))
-            total = term if total is None else fmap(jnp.add, total, term)
-        return total
-
-    def around_own(v):
-        main, side = v.main, v.side[:rows]
-        own = main[:, :rows]
-        below = jnp.concatenate([own[1:], jnp.zeros_like(own[:1])], axis=0)
-        above = jnp.concatenate([jnp.zeros_like(own[:1]), own[:-1]], axis=0)
-        moved = (
-            (below, above),
-            (row_roll(main, -1)[:, :rows], row_roll(main, 1)[:, :rows]),
-            (y_next_main(own, side), y_prev_main(own, side)),
-        )
-        return add(*[c.main[:, :rows] * n + b.main[:, :rows] * p for c, b, (n, p) in zip(coefs, before, moved)])
+    (mob,) = build(lambda i: [mobility(s.at(i))], nb)
+    scalings = (VERTICAL, 1.0, 1.0)
+    coefs = [Field([], None) for _ in NEXT]
+    before = [Field([], None) for _ in NEXT]
+    diag, inverse = Field([], None), Field([], None)
+
+    def face(i):
+        return [
+            coefficient(sc)(k.at(i), nxt(k, i), mob.at(i), nxt(mob, i)) for nxt, sc in zip(NEXT, scalings)
+        ]
+
+    def centre(i):
+        sides = [prv(c, i) for prv, c in zip(PREV, coefs)]
+        d = add(STORAGE, *[c.at(i) for c in coefs], *sides)
+        return sides, d, inverted(d)
+
+    for c, value in zip(coefs, face(None)):
+        c.side = value
+    for i in range(nb):
+        for c, value in zip(coefs, face(i)):
+            c.blocks.append(value)
+        sides, d, r = centre(i)
+        for c, value in zip(before, sides):
+            c.blocks.append(value)
+        diag.blocks.append(d)
+        inverse.blocks.append(r)
+    sides, diag.side, inverse.side = centre(None)
+    for c, value in zip(before, sides):
+        c.side = value
+
+    def around(v, i):
+        return add(*[
+            c.at(i) * nxt(v, i) + b.at(i) * prv(v, i) for nxt, prv, c, b in zip(NEXT, PREV, coefs, before)
+        ])
 
     arrive(1)
     x0, q = field(2), field(3)
-    r0 = fmap(lambda q, x, d, a: q + STORAGE * x - (d * x - a), q, x0, diag, around(x0))
-    u0 = fmap(jnp.multiply, r0, inverse)
-    v0 = fmap(lambda d, u, a: d * u - a, diag, u0, around(u0))
-    u1 = fmap(jnp.multiply, v0, inverse)
-    own_v1 = diag.main[:, :rows] * u1.main[:, :rows] - around_own(u1)
-
-    def own(f):
-        return f.main[:, :rows]
-
-    pairs = ((own(r0), own(u0)), (own(u0), own(v0)), (own(v0), own(u1)), (own(u1), own_v1))
+    (u0,) = build(
+        lambda i: [(q.at(i) + STORAGE * x0.at(i) - (diag.at(i) * x0.at(i) - around(x0, i))) * inverse.at(i)], nb
+    )
+    (u1,) = build(lambda i: [u0.at(i) - around(u0, i) * inverse.at(i)], nb)
+    sums = [0.0] * 4
+    for i in range(nb):
+        d, a, b = [f.blocks[i][:, :rows] for f in (diag, u0, u1)]
+        da, db = d * a, d * b
+        image = db - around(u1, i)[:, :rows]
+        for n, value in enumerate((da * a, da * b, db * b, b * image)):
+            sums[n] = sums[n] + jnp.sum(value, axis=0)
+
     tile_row = iota((rows, lanes), 0)
     part = jnp.zeros((rows, lanes), jnp.float32)
-    for i, (left, other) in enumerate(pairs):
-        part = jnp.where(tile_row == i, jnp.sum(jnp.sum(left * other, axis=0), axis=0, keepdims=True), part)
+    for i, value in enumerate(sums):
+        part = jnp.where(tile_row == i, jnp.sum(value, axis=0, keepdims=True), part)
 
     late_send[...] = own(u1)
 
@@ -354,20 +371,17 @@
     for off in range(1, count):
         share_copy(off, off, 1).start()
 
-    inject = fmap(lambda v: jnp.maximum(v, 0.0), q)
-    produce = fmap(lambda v: jnp.minimum(v, 0.0), q)
-
-    def shares(current):
-        frac = fmap(fraction, current)
-        gained = fmap(lambda i, o, f: i + o * f, inject, produce, frac)
-        return frac, gained, [nxt(frac) for nxt in NEXT]
+    def gained(i, frac):
+        return jnp.maximum(q.at(i), 0.0) + jnp.minimum(q.at(i), 0.0) * frac
 
     for dx in (-1, 1):
         @pl.when(has(dx, 0))
         def _():
             late_copy(dx).start()
 
-    first_shares = shares(s)
+    (frac,) = build(lambda i: [fraction(s.at(i))], nb)
+    (gain,) = build(lambda i: [gained(i, frac.at(i))], nb)
+    after = build(lambda i: [nxt(frac, i) for nxt in NEXT], nb)
     for dx in (-1, 1):
         @pl.when(has(-dx, 0))
         def _():
@@ -377,7 +391,17 @@
     late_row = iota(late.shape, 1)
     taken = ((late_row == 1) & (gx + 1 < nx)) | ((late_row == rows - 2) & (gx > 0))
     u1 = Field(
-        jnp.concatenate([own(u1), jnp.where(taken, late, u1.main[:, rows:])], axis=1), u1.side
+        [
+            jnp.concatenate(
+                [
+                    b[:, :rows],
+                    jnp.where(taken[i * BLOCK : (i + 1) * BLOCK], late[i * BLOCK : (i + 1) * BLOCK], b[:, rows:]),
+                ],
+                axis=1,
+            )
+            for i, b in enumerate(u1.blocks)
+        ],
+        u1.side,
     )
     share_copy(1, 1, count - 1).wait_recv()
     total = jnp.sum(slots[...], axis=0, keepdims=True)
@@ -391,18 +415,44 @@
     weight0 = step0 + step1 * (1.0 + conjugacy)
     weight1 = -step1 * step0
 
-    pressure = fmap(lambda x, a, b: x + weight0 * a + weight1 * b, x0, u0, u1)
-    p_out[...] = own(pressure)
-    flows = [fmap(lambda c, a, b: c * (a - b), c, pressure, nxt(pressure)) for nxt, c in zip(NEXT, coefs)]
-    def transport(current, share):
-        frac, total, after = share
-        for prv, flow, nf in zip(PREV, flows, after):
-            water = fmap(lambda w, a, b: w * jnp.where(w > 0.0, a, b), flow, frac, nf)
-            total = fmap(lambda t, w, p: t - (w - p), total, water, prv(water))
-        return fmap(lambda c, t: c + STEP * t, current, total)
-
-    first = transport(s, first_shares)
-    s_out[...] = own(transport(first, shares(first)))
+    (pressure,) = build(lambda i: [x0.at(i) + weight0 * u0.at(i) + weight1 * u1.at(i)], nb)
+    flows = [Field([], None) for _ in NEXT]
+
+    def flux(i):
+        return [c.at(i) * (pressure.at(i) - nxt(pressure, i)) for nxt, c in zip(NEXT, coefs)]
+
+    def water_at(i, frac, nexts):
+        return [
+            f.at(i) * jnp.where(f.at(i) > 0.0, frac.at(i), n) for f, n in zip(flows, nexts)
+        ]
+
+    def moved(i, current, gain, water):
+        return current + STEP * add(gain, *[prv(w, i) - w.at(i) for prv, w in zip(PREV, water)])
+
+    water = [Field([], None) for _ in NEXT]
+    first = Field([], None)
+    for f, value in zip(flows, flux(None)):
+        f.side = value
+    for w, value in zip(water, water_at(None, frac, [n.side for n in after])):
+        w.side = value
+    for i in range(nb):
+        p_out[i * BLOCK : (i + 1) * BLOCK] = pressure.blocks[i][:, :rows]
+        for f, value in zip(flows, flux(i)):
+            f.blocks.append(value)
+        for w, value in zip(water, water_at(i, frac, [n.blocks[i] for n in after])):
+            w.blocks.append(value)
+        first.blocks.append(moved(i, s.blocks[i], gain.blocks[i], water))
+    first.side = moved(None, s.side, gain.side, water)
+
+    (frac,) = build(lambda i: [fraction(first.at(i))], nb)
+    water = [Field([], None) for _ in NEXT]
+    for w, value in zip(water, water_at(None, frac, [nxt(frac, None) for nxt in NEXT])):
+        w.side = value
+    for i in range(nb):
+        for w, value in zip(water, water_at(i, frac, [nxt(frac, i) for nxt in NEXT])):
+            w.blocks.append(value)
+        second = moved(i, first.blocks[i], gained(i, frac.blocks[i]), water)
+        s_out[i * BLOCK : (i + 1) * BLOCK] = second[:, :rows]
 
     for dx in (-1, 1):
         @pl.when(has(dx, 0))
@@ -423,7 +473,7 @@
 def local(nx, ny, permeability, saturation, pressure_old, source):
     shape = source.shape
     depth, rows, lanes = shape
-    assert permeability.shape[0] == 1 and depth * 2 * HALO == lanes and rows == 2 * HALO
+    assert permeability.shape[0] == 1 and depth % BLOCK == 0 and depth * 2 * HALO == lanes and rows == 2 * HALO
     wide = rows + 2 * HALO
     f32 = jnp.float32
     dma = pltpu.SemaphoreType.DMA

time: 20.4 us -> 20.4 us (level)
  no operation moved by 1% of the time
where the time goes in v5:
time: 20.4 us; the launch traced here: 20.3 us
  Pallas kernels  18.4 us (90%)
  local copies, waits for them, and re-layouts  1.26 us (6%)
  between operations  0.64 us (3%)
    pallas_call x1, Pallas kernels, local(): pl.pallas_call(functools.partial(kernel, nx, ny), out_shape=[jax.ShapeDty...  18.4 us
    unnamed x2, local copies, waits for them, and re-layouts  1.26 us

profile of v5, /device:TPU:0, one launch (start us, length us, event | category | flops | bytes accessed | tf_op | source)
XLA Modules:
  0.0 20.3 jit_solution(4866761948874310161)
XLA Ops:
  0.6 18.4 %shard_map.59 = (f32[16,8,128]{2,1,0:T(8,128)S(1)}, f32[16,8,128]{2,1,0:T(8,128)S(1)}) custom-call(f32[16,8,128]{2,1,0:T(8,128)} %bitcast.7, f32[16,8,128]{2,1,0:T(8,128)} %bitcast.8, f32[16,8,128]{2,1,0:T(8,128)} %bitcast.9, f32[16,8,128]{2,1,0:T(8,128)} %q_in.1), custom_call_target="tpu_custom_call" | custom-call | tf_op jit(solution)/shard_map/pallas_call | solution.py:480
  19.0 0.6 %copy.8 = f32[1,16,8,128]{3,2,1,0:T(8,128)} copy(f32[1,16,8,128]{3,2,1,0:T(8,128)S(1)} %bitcast.6) | data formatting | bytes 131072
  19.6 0.6 %copy.9 = f32[1,16,8,128]{3,2,1,0:T(8,128)} copy(f32[1,16,8,128]{3,2,1,0:T(8,128)S(1)} %bitcast.5) | data formatting | bytes 131072

commit v6 on v5

--- a/solution.py
+++ b/solution.py
@@ -148,7 +148,7 @@
 
 
 def kernel(nx, ny, k_in, s_in, x_in, q_in, p_out, s_out, main_ref, pack_ref, side_ref, slots,
-           late_send, late_recv, load_sem, xsend, xrecv, psend, precv, rsend, rrecv, ready, lsem, lrecv):
+           late_send, late_recv, early_send, early_recv, load_sem, xsend, xrecv, psend, precv, rsend, rrecv, ready, lsem, lrecv, esem, erecv):
     gx, gy = lax.axis_index("gx"), lax.axis_index("gy")
     ins = (k_in, s_in, x_in, q_in)
     rows = k_in.shape[1]
@@ -184,7 +184,7 @@
 
         expected = expected + has(dx, dy).astype(jnp.int32)
 
-    reach = (HALO - 1, HALO - 1, HALO - 1, HALO - 2)
+    reach = (2, 2, 2, 1)
 
     def edge_rows(dx, width):
         return pl.ds(0, width) if dx < 0 else pl.ds(rows - width, width)
@@ -207,66 +207,73 @@
             if i // 2 in halves
         ]
 
-    def y_copy(half, dx, dy):
-        number = half * 6 + (dx + 1) * 2 + (dy + 1) // 2
+    def y_copy(dx, dy):
+        number = (dx + 1) * 2 + (dy + 1) // 2
         from_rows = to_rows = pl.ds(0, rows)
         if dx:
-            from_rows, to_rows = edge_rows(dx, HALO - 1), halo_rows(dx, HALO - 1)
-        arrays = pl.ds(2 * half, 2)
+            from_rows, to_rows = edge_rows(dx, reach[0]), halo_rows(dx, reach[0])
         return pltpu.make_async_remote_copy(
-            src_ref=pack_ref.at[arrays, from_rows],
-            dst_ref=side_ref.at[(1 - dy) // 2, arrays, to_rows],
+            src_ref=pack_ref.at[:, from_rows],
+            dst_ref=side_ref.at[(1 - dy) // 2, :, to_rows],
             send_sem=psend.at[number],
             recv_sem=precv.at[number],
             device_id=at(dx, dy),
             device_id_type=MESH,
         )
 
-    def late_copy(dx):
+    def line_copy(dx, src, dst, send, recv):
         line = pl.ds(1, 1) if dx < 0 else pl.ds(rows - 2, 1)
         d = (dx + 1) // 2
         return pltpu.make_async_remote_copy(
-            src_ref=late_send.at[:, line],
-            dst_ref=late_recv.at[:, line],
-            send_sem=lsem.at[d],
-            recv_sem=lrecv.at[d],
+            src_ref=src.at[:, line],
+            dst_ref=dst.at[:, line],
+            send_sem=send.at[d],
+            recv_sem=recv.at[d],
             device_id=at(dx, 0),
             device_id_type=MESH,
         )
 
+    def early_copy(dx):
+        return line_copy(dx, early_send, early_recv, esem, erecv)
+
+    def late_copy(dx):
+        return line_copy(dx, late_send, late_recv, lsem, lrecv)
+
     y_moves = [(0, 1), (0, -1)] + diagonals
 
+    for i in range(len(ins)):
+        loads[i].wait()
+        pack_ref[i] = packed(main_ref[i, :, 0:rows, :])
+
     pl.semaphore_wait(barrier, expected)
-    for dx in (-1, 1):
-        @pl.when(has(dx, 0))
-        def _():
-            for copy in x_copies(dx):
-                copy.start()
+    for dx, dy in y_moves:
+        @pl.when(has(dx, dy))
+        def _():
+            y_copy(dx, dy).start()
+
+    for half in range(2):
+        for dx in (-1, 1):
+            @pl.when(has(dx, 0))
+            def _():
+                for copy in x_copies(dx, (half,)):
+                    copy.start()
 
     for off in range(1, nx):
         pl.semaphore_signal(ready, inc=1, device_id={"gx": lax.rem(gx + off, nx), "gy": gy}, device_id_type=MESH)
 
-    for half in range(2):
-        for i in (2 * half, 2 * half + 1):
-            loads[i].wait()
-            pack_ref[i] = packed(main_ref[i, :, 0:rows, :])
-        for dx, dy in y_moves:
-            @pl.when(has(dx, dy))
+    def arrive_y(moves):
+        for dx, dy in moves:
+            @pl.when(has(-dx, -dy))
             def _():
-                y_copy(half, dx, dy).start()
-
-    def arrive(half):
+                y_copy(dx, dy).wait_recv()
+
+    def arrive_x(half):
         for dx in (-1, 1):
             @pl.when(has(-dx, 0))
             def _():
                 for copy in x_copies(dx, (half,)):
                     copy.wait_recv()
 
-        for dx, dy in y_moves:
-            @pl.when(has(-dx, -dy))
-            def _():
-                y_copy(half, dx, dy).wait_recv()
-
     lanes = k_in.shape[2]
     depth = k_in.shape[0]
     row = iota((wide, lanes), 0)
@@ -275,63 +282,109 @@
 
     nb = depth // BLOCK
 
-    def field(i):
+    def field(i, high):
+        at_row, at_right = row[:high], right[:high]
         inside = (
-            (row < rows)
-            | ((row < rows + reach[i]) & (gx + 1 < nx))
-            | ((row >= wide - reach[i]) & (gx > 0))
+            (at_row < rows)
+            | ((at_row < rows + reach[i]) & (gx + 1 < nx))
+            | ((at_row >= wide - reach[i]) & (gx > 0))
         )
-        inside_right = right & inside & (gy + 1 < ny)
-        inside_left = jnp.logical_not(right) & inside & (gy > 0)
-        blocks = [jnp.where(inside[None], main_ref[i, n * BLOCK : (n + 1) * BLOCK], 0.0) for n in range(nb)]
-        side = jnp.where(inside_right, side_ref[1, i], jnp.where(inside_left, side_ref[0, i], 0.0))
+        inside_right = at_right & inside & (gy + 1 < ny)
+        inside_left = jnp.logical_not(at_right) & inside & (gy > 0)
+        blocks = [main_ref[i, n * BLOCK : (n + 1) * BLOCK, 0:high] for n in range(nb)]
+        if high > rows:
+            blocks = [jnp.where(inside[None], b, 0.0) for b in blocks]
+        side = jnp.where(
+            inside_right, side_ref[1, i, 0:high], jnp.where(inside_left, side_ref[0, i, 0:high], 0.0)
+        )
         return Field(blocks, side)
 
     def own(f):
         return jnp.concatenate([b[:, :rows] for b in f.blocks], axis=0)
 
-    arrive(0)
-    k, s = field(0), field(1)
-    (mob,) = build(lambda i: [mobility(s.at(i))], nb)
-    scalings = (VERTICAL, 1.0, 1.0)
-    coefs = [Field([], None) for _ in NEXT]
-    before = [Field([], None) for _ in NEXT]
-    diag, inverse = Field([], None), Field([], None)
-
-    def face(i):
-        return [
-            coefficient(sc)(k.at(i), nxt(k, i), mob.at(i), nxt(mob, i)) for nxt, sc in zip(NEXT, scalings)
-        ]
-
-    def centre(i):
-        sides = [prv(c, i) for prv, c in zip(PREV, coefs)]
-        d = add(STORAGE, *[c.at(i) for c in coefs], *sides)
-        return sides, d, inverted(d)
-
-    for c, value in zip(coefs, face(None)):
-        c.side = value
-    for i in range(nb):
-        for c, value in zip(coefs, face(i)):
-            c.blocks.append(value)
-        sides, d, r = centre(i)
+    def stencil(k, s):
+        (mob,) = build(lambda i: [mobility(s.at(i))], nb)
+        scalings = (VERTICAL, 1.0, 1.0)
+        coefs = [Field([], None) for _ in NEXT]
+        before = [Field([], None) for _ in NEXT]
+        diag, inverse = Field([], None), Field([], None)
+
+        def face(i):
+            return [
+                coefficient(sc)(k.at(i), nxt(k, i), mob.at(i), nxt(mob, i)) for nxt, sc in zip(NEXT, scalings)
+            ]
+
+        def centre(i):
+            sides = [prv(c, i) for prv, c in zip(PREV, coefs)]
+            d = add(STORAGE, *[c.at(i) for c in coefs], *sides)
+            return sides, d, inverted(d)
+
+        for c, value in zip(coefs, face(None)):
+            c.side = value
+        for i in range(nb):
+            for c, value in zip(coefs, face(i)):
+                c.blocks.append(value)
+            sides, d, r = centre(i)
+            for c, value in zip(before, sides):
+                c.blocks.append(value)
+            diag.blocks.append(d)
+            inverse.blocks.append(r)
+        sides, diag.side, inverse.side = centre(None)
         for c, value in zip(before, sides):
-            c.blocks.append(value)
-        diag.blocks.append(d)
-        inverse.blocks.append(r)
-    sides, diag.side, inverse.side = centre(None)
-    for c, value in zip(before, sides):
-        c.side = value
-
-    def around(v, i):
-        return add(*[
-            c.at(i) * nxt(v, i) + b.at(i) * prv(v, i) for nxt, prv, c, b in zip(NEXT, PREV, coefs, before)
-        ])
-
-    arrive(1)
-    x0, q = field(2), field(3)
-    (u0,) = build(
-        lambda i: [(q.at(i) + STORAGE * x0.at(i) - (diag.at(i) * x0.at(i) - around(x0, i))) * inverse.at(i)], nb
-    )
+            c.side = value
+        return coefs, before, diag, inverse
+
+    def around_in(coefs, before):
+        def around(v, i):
+            return add(*[
+                c.at(i) * nxt(v, i) + b.at(i) * prv(v, i)
+                for nxt, prv, c, b in zip(NEXT, PREV, coefs, before)
+            ])
+
+        return around
+
+    def start_field(x0, q, around, diag, inverse):
+        return build(
+            lambda i: [(q.at(i) + STORAGE * x0.at(i) - (diag.at(i) * x0.at(i) - around(x0, i))) * inverse.at(i)],
+            nb,
+        )[0]
+
+    arrive_y(y_moves[:2])
+    coefs, before, diag, inverse = stencil(field(0, rows), field(1, rows))
+    u0 = start_field(field(2, rows), field(3, rows), around_in(coefs, before), diag, inverse)
+    for i, b in enumerate(u0.blocks):
+        early_send[i * BLOCK : (i + 1) * BLOCK] = b
+    early_send[depth] = u0.side
+    for dx in (-1, 1):
+        @pl.when(has(dx, 0))
+        def _():
+            early_copy(dx).start()
+
+    line_row = iota((rows, lanes), 0)
+    taken = ((line_row == 1) & (gx + 1 < nx)) | ((line_row == rows - 2) & (gx > 0))
+
+    def patched(value, ref, planes):
+        cut = value[..., :rows, :], value[..., rows:, :]
+        return jnp.concatenate([cut[0], jnp.where(taken, ref[planes], cut[1])], axis=-2)
+
+    def patch(f, ref):
+        f.blocks = [patched(b, ref, slice(i * BLOCK, (i + 1) * BLOCK)) for i, b in enumerate(f.blocks)]
+
+    arrive_y(y_moves[2:])
+    arrive_x(0)
+    k, s = field(0, wide), field(1, wide)
+    coefs, before, diag, inverse = stencil(k, s)
+    around = around_in(coefs, before)
+    arrive_x(1)
+    x0, q = field(2, wide), field(3, wide)
+    u0 = start_field(x0, q, around, diag, inverse)
+    for dx in (-1, 1):
+        @pl.when(has(-dx, 0))
+        def _():
+            early_copy(dx).wait_recv()
+
+    patch(u0, early_recv)
+    u0.side = patched(u0.side, early_recv, depth)
     (u1,) = build(lambda i: [u0.at(i) - around(u0, i) * inverse.at(i)], nb)
     sums = [0.0] * 4
     for i in range(nb):
@@ -387,22 +440,7 @@
         def _():
             late_copy(dx).wait_recv()
 
-    late = late_recv[...]
-    late_row = iota(late.shape, 1)
-    taken = ((late_row == 1) & (gx + 1 < nx)) | ((late_row == rows - 2) & (gx > 0))
-    u1 = Field(
-        [
-            jnp.concatenate(
-                [
-                    b[:, :rows],
-                    jnp.where(taken[i * BLOCK : (i + 1) * BLOCK], late[i * BLOCK : (i + 1) * BLOCK], b[:, rows:]),
-                ],
-                axis=1,
-            )
-            for i, b in enumerate(u1.blocks)
-        ],
-        u1.side,
-    )
+    patch(u1, late_recv)
     share_copy(1, 1, count - 1).wait_recv()
     total = jnp.sum(slots[...], axis=0, keepdims=True)
     sums = jnp.sum(jnp.where(mine, total, 0.0), axis=1, keepdims=True)
@@ -459,13 +497,13 @@
         def _():
             for copy in x_copies(dx):
                 copy.wait_send()
+            early_copy(dx).wait_send()
             late_copy(dx).wait_send()
 
     for dx, dy in y_moves:
         @pl.when(has(dx, dy))
         def _():
-            for half in range(2):
-                y_copy(half, dx, dy).wait_send()
+            y_copy(dx, dy).wait_send()
 
     share_copy(1, 1, count - 1).wait_send()
 
@@ -489,14 +527,18 @@
             pltpu.VMEM((nx * ny, lanes), f32),
             pltpu.VMEM(shape, f32),
             pltpu.VMEM(shape, f32),
+            pltpu.VMEM((depth + 1, rows, lanes), f32),
+            pltpu.VMEM((depth + 1, rows, lanes), f32),
             dma((4,)),
             dma((8,)),
             dma((8,)),
-            dma((12,)),
-            dma((12,)),
+            dma((6,)),
+            dma((6,)),
             dma,
             dma,
             pltpu.SemaphoreType.REGULAR,
+            dma((2,)),
+            dma((2,)),
             dma((2,)),
             dma((2,)),
         ],

time: 20.4 us -> 19.2 us (0.941)
  Pallas kernels: 18.4 us -> 17.1 us
    pallas_call x1, Pallas kernels: 18.4 us -> 17.1 us  [local(): pl.pallas_call(functools.partial(kernel, nx, ny), out_shape=[jax.ShapeDty...]
where the time goes in v6:
time: 19.2 us; the launch traced here: 19 us
  Pallas kernels  17.1 us (89%)
  local copies, waits for them, and re-layouts  1.26 us (7%)
  between operations  0.64 us (3%)
    pallas_call x1, Pallas kernels, local(): pl.pallas_call(functools.partial(kernel, nx, ny), out_shape=[jax.ShapeDty...  17.1 us
    unnamed x2, local copies, waits for them, and re-layouts  1.26 us

profile of v6, /device:TPU:0, one launch (start us, length us, event | category | flops | bytes accessed | tf_op | source)
XLA Modules:
  0.0 19.0 jit_solution(2118642399530248796)
XLA Ops:
  0.6 17.1 %shard_map.59 = (f32[16,8,128]{2,1,0:T(8,128)S(1)}, f32[16,8,128]{2,1,0:T(8,128)S(1)}) custom-call(f32[16,8,128]{2,1,0:T(8,128)} %bitcast.7, f32[16,8,128]{2,1,0:T(8,128)} %bitcast.8, f32[16,8,128]{2,1,0:T(8,128)} %bitcast.9, f32[16,8,128]{2,1,0:T(8,128)} %q_in.1), custom_call_target="tpu_custom_call" | custom-call | tf_op jit(solution)/shard_map/pallas_call | solution.py:518
  17.8 0.6 %copy.8 = f32[1,16,8,128]{3,2,1,0:T(8,128)} copy(f32[1,16,8,128]{3,2,1,0:T(8,128)S(1)} %bitcast.6) | data formatting | bytes 131072
  18.4 0.6 %copy.9 = f32[1,16,8,128]{3,2,1,0:T(8,128)} copy(f32[1,16,8,128]{3,2,1,0:T(8,128)S(1)} %bitcast.5) | data formatting | bytes 131072

commit v7 on v6

--- a/solution.py
+++ b/solution.py
@@ -101,6 +101,28 @@
     r = pl.reciprocal(v, approx=True)
     r = r * (2.0 - v * r)
     return r * (2.0 - v * r)
+
+
+def y_both(f):
+    width = 2 * HALO
+    side = f.side
+    lane = iota(side.shape, 1)
+    column = lane % width
+    edges = jnp.where(column == 0, lane_roll(side, 1 - width), lane_roll(side, -1))
+    ends = jnp.zeros_like(side)
+    nexts, prevs = [], []
+    for i, b in enumerate(f.blocks):
+        put = jnp.stack([lane_roll(edges, -width * (i * BLOCK + j)) for j in range(BLOCK)], axis=0)
+        at_lane = iota(b.shape, 2)
+        up = lane_roll(b, 1)
+        nexts.append(jnp.where(at_lane == b.shape[2] - 1, put, lane_roll(b, -1)))
+        prevs.append(jnp.where(at_lane == 0, put, up))
+        for j in range(BLOCK):
+            z = i * BLOCK + j
+            ends = jnp.where(lane // width == z, lane_roll(up[j], width * z), ends)
+    side_next = jnp.where(column == width - 1, lane_roll(ends, width - 2), lane_roll(side, -1))
+    side_prev = jnp.where(column == 0, ends, lane_roll(side, 1))
+    return Field(nexts, side_next), Field(prevs, side_prev)
 
 
 def mobility(s):
@@ -147,7 +169,7 @@
     return out
 
 
-def kernel(nx, ny, k_in, s_in, x_in, q_in, p_out, s_out, main_ref, pack_ref, side_ref, slots,
+def kernel(nx, ny, k_in, s_in, x_in, q_in, out_ref, main_ref, pack_ref, side_ref, slots,
            late_send, late_recv, early_send, early_recv, load_sem, xsend, xrecv, psend, precv, rsend, rrecv, ready, lsem, lrecv, esem, erecv):
     gx, gy = lax.axis_index("gx"), lax.axis_index("gy")
     ins = (k_in, s_in, x_in, q_in)
@@ -302,56 +324,86 @@
     def own(f):
         return jnp.concatenate([b[:, :rows] for b in f.blocks], axis=0)
 
-    def stencil(k, s):
+    def zy_faces(k, s):
         (mob,) = build(lambda i: [mobility(s.at(i))], nb)
-        scalings = (VERTICAL, 1.0, 1.0)
-        coefs = [Field([], None) for _ in NEXT]
-        before = [Field([], None) for _ in NEXT]
-        diag, inverse = Field([], None), Field([], None)
+        coefs = [Field([], None) for _ in range(2)]
+        before = [Field([], None) for _ in range(2)]
 
         def face(i):
             return [
-                coefficient(sc)(k.at(i), nxt(k, i), mob.at(i), nxt(mob, i)) for nxt, sc in zip(NEXT, scalings)
+                coefficient(sc)(k.at(i), nxt(k, i), mob.at(i), nxt(mob, i))
+                for nxt, sc in ((z_next, VERTICAL), (y_next, 1.0))
             ]
 
-        def centre(i):
-            sides = [prv(c, i) for prv, c in zip(PREV, coefs)]
-            d = add(STORAGE, *[c.at(i) for c in coefs], *sides)
-            return sides, d, inverted(d)
+        def behind(i):
+            return [prv(c, i) for prv, c in zip((z_prev, y_prev), coefs)]
 
         for c, value in zip(coefs, face(None)):
             c.side = value
         for i in range(nb):
             for c, value in zip(coefs, face(i)):
                 c.blocks.append(value)
-            sides, d, r = centre(i)
-            for c, value in zip(before, sides):
+            for c, value in zip(before, behind(i)):
                 c.blocks.append(value)
-            diag.blocks.append(d)
-            inverse.blocks.append(r)
-        sides, diag.side, inverse.side = centre(None)
-        for c, value in zip(before, sides):
+        for c, value in zip(before, behind(None)):
             c.side = value
-        return coefs, before, diag, inverse
-
-    def around_in(coefs, before):
-        def around(v, i):
-            return add(*[
-                c.at(i) * nxt(v, i) + b.at(i) * prv(v, i)
-                for nxt, prv, c, b in zip(NEXT, PREV, coefs, before)
-            ])
-
-        return around
-
-    def start_field(x0, q, around, diag, inverse):
+        return mob, coefs, before
+
+    def x_faces(k, mob):
+        (c,) = build(
+            lambda i: [coefficient(1.0)(k.at(i), x_next(k, i), mob.at(i), x_next(mob, i))], nb
+        )
+        (b,) = build(lambda i: [x_prev(c, i)], nb)
+        return c, b
+
+    def zy_diag(coefs, before):
+        return build(lambda i: [add(STORAGE, *[f.at(i) for f in coefs + before])], nb)[0]
+
+    def zy_around(v, coefs, before):
+        ahead, back = y_both(v)
         return build(
-            lambda i: [(q.at(i) + STORAGE * x0.at(i) - (diag.at(i) * x0.at(i) - around(x0, i))) * inverse.at(i)],
+            lambda i: [
+                coefs[0].at(i) * z_next(v, i)
+                + before[0].at(i) * z_prev(v, i)
+                + coefs[1].at(i) * ahead.at(i)
+                + before[1].at(i) * back.at(i)
+            ],
             nb,
         )[0]
 
+    def x_around(v, c, b, i):
+        return c.at(i) * x_next(v, i) + b.at(i) * x_prev(v, i)
+
+    def whole_diag(partial, c, b):
+        return build(lambda i: (lambda d: [d, inverted(d)])(partial.at(i) + c.at(i) + b.at(i)), nb)
+
+    def start_field(x0, q, partial, c, b, diag, inverse):
+        return build(
+            lambda i: [
+                (q.at(i) + STORAGE * x0.at(i) - (diag.at(i) * x0.at(i) - (partial.at(i) + x_around(x0, c, b, i))))
+                * inverse.at(i)
+            ],
+            nb,
+        )[0]
+
+    def lower(f):
+        return Field([b[:, rows:] for b in f.blocks], f.side[rows:])
+
+    def join(f, g):
+        return Field(
+            [jnp.concatenate([a, b], axis=1) for a, b in zip(f.blocks, g.blocks)],
+            jnp.concatenate([f.side, g.side], axis=0),
+        )
+
     arrive_y(y_moves[:2])
-    coefs, before, diag, inverse = stencil(field(0, rows), field(1, rows))
-    u0 = start_field(field(2, rows), field(3, rows), around_in(coefs, before), diag, inverse)
+    k, s = field(0, rows), field(1, rows)
+    own_mob, own_coefs, own_before = zy_faces(k, s)
+    own_diag = zy_diag(own_coefs, own_before)
+    x_coef, x_before = x_faces(k, own_mob)
+    diag, inverse = whole_diag(own_diag, x_coef, x_before)
+    x0 = field(2, rows)
+    own_around = zy_around(x0, own_coefs, own_before)
+    u0 = start_field(x0, field(3, rows), own_around, x_coef, x_before, diag, inverse)
     for i, b in enumerate(u0.blocks):
         early_send[i * BLOCK : (i + 1) * BLOCK] = b
     early_send[depth] = u0.side
@@ -373,11 +425,17 @@
     arrive_y(y_moves[2:])
     arrive_x(0)
     k, s = field(0, wide), field(1, wide)
-    coefs, before, diag, inverse = stencil(k, s)
-    around = around_in(coefs, before)
+    halo_mob, halo_coefs, halo_before = zy_faces(lower(k), lower(s))
+    halo_diag = zy_diag(halo_coefs, halo_before)
+    x_coef, x_before = x_faces(k, join(own_mob, halo_mob))
+    diag, inverse = whole_diag(join(own_diag, halo_diag), x_coef, x_before)
+    z_coef, y_coef = [join(f, g) for f, g in zip(own_coefs, halo_coefs)]
+    z_before, y_before = [join(f, g) for f, g in zip(own_before, halo_before)]
+    coefs = (z_coef, x_coef, y_coef)
     arrive_x(1)
     x0, q = field(2, wide), field(3, wide)
-    u0 = start_field(x0, q, around, diag, inverse)
+    partial = join(own_around, zy_around(lower(x0), halo_coefs, halo_before))
+    u0 = start_field(x0, q, partial, x_coef, x_before, diag, inverse)
     for dx in (-1, 1):
         @pl.when(has(-dx, 0))
         def _():
@@ -385,12 +443,18 @@
 
     patch(u0, early_recv)
     u0.side = patched(u0.side, early_recv, depth)
-    (u1,) = build(lambda i: [u0.at(i) - around(u0, i) * inverse.at(i)], nb)
+    def around(v):
+        partial = zy_around(v, (z_coef, y_coef), (z_before, y_before))
+        return lambda i: partial.at(i) + x_around(v, x_coef, x_before, i)
+
+    near = around(u0)
+    (u1,) = build(lambda i: [u0.at(i) - near(i) * inverse.at(i)], nb)
+    near = around(u1)
     sums = [0.0] * 4
     for i in range(nb):
         d, a, b = [f.blocks[i][:, :rows] for f in (diag, u0, u1)]
         da, db = d * a, d * b
-        image = db - around(u1, i)[:, :rows]
+        image = db - near(i)[:, :rows]
         for n, value in enumerate((da * a, da * b, db * b, b * image)):
             sums[n] = sums[n] + jnp.sum(value, axis=0)
 
@@ -474,7 +538,7 @@
     for w, value in zip(water, water_at(None, frac, [n.side for n in after])):
         w.side = value
     for i in range(nb):
-        p_out[i * BLOCK : (i + 1) * BLOCK] = pressure.blocks[i][:, :rows]
+        out_ref[0, i * BLOCK : (i + 1) * BLOCK] = pressure.blocks[i][:, :rows]
         for f, value in zip(flows, flux(i)):
             f.blocks.append(value)
         for w, value in zip(water, water_at(i, frac, [n.blocks[i] for n in after])):
@@ -490,7 +554,7 @@
         for w, value in zip(water, water_at(i, frac, [nxt(frac, i) for nxt in NEXT])):
             w.blocks.append(value)
         second = moved(i, first.blocks[i], gained(i, frac.blocks[i]), water)
-        s_out[i * BLOCK : (i + 1) * BLOCK] = second[:, :rows]
+        out_ref[1, i * BLOCK : (i + 1) * BLOCK] = second[:, :rows]
 
     for dx in (-1, 1):
         @pl.when(has(dx, 0))
@@ -517,9 +581,9 @@
     dma = pltpu.SemaphoreType.DMA
     outs = pl.pallas_call(
         functools.partial(kernel, nx, ny),
-        out_shape=[jax.ShapeDtypeStruct(shape, f32)] * 2,
+        out_shape=jax.ShapeDtypeStruct((2,) + shape, f32),
         in_specs=[pl.BlockSpec(memory_space=pltpu.HBM)] * 4,
-        out_specs=[pl.BlockSpec(memory_space=pltpu.VMEM)] * 2,
+        out_specs=pl.BlockSpec(memory_space=pltpu.VMEM),
         scratch_shapes=[
             pltpu.VMEM((4, depth, wide, lanes), f32),
             pltpu.VMEM((4, rows, lanes), f32),
@@ -546,7 +610,7 @@
             collective_id=0, has_side_effects=True, vmem_limit_bytes=32 * 1024 * 1024
         ),
     )(*[pltpu.with_memory_space_constraint(v, pltpu.HBM) for v in (permeability[0], saturation[0], pressure_old[0], source)])
-    return outs[0][None], outs[1][None]
+    return outs[:1], outs[1:]
 
 
 def solution(mesh):

time: 19.2 us -> 18.6 us (0.969)
  local copies, waits for them, and re-layouts: 1.26 us -> 0.66 us
    unnamed x2 -> x0, local copies, waits for them, and re-layouts: 1.26 us -> none
    slice x0 -> x1, local copies, waits for them, and re-layouts: none -> 0.66 us  [local(): return (outs[:1], outs[1:])]
where the time goes in v7:
time: 18.6 us; the launch traced here: 18.4 us
  Pallas kernels  17.1 us (92%)
  local copies, waits for them, and re-layouts  0.66 us (4%)
  between operations  0.64 us (3%)
    pallas_call x1, Pallas kernels, local(): pl.pallas_call(functools.partial(kernel, nx, ny), out_shape=jax.ShapeDtyp...  17.1 us
    slice x1, local copies, waits for them, and re-layouts, local(): return (outs[:1], outs[1:])  0.66 us

profile of v7, /device:TPU:0, one launch (start us, length us, event | category | flops | bytes accessed | tf_op | source)
XLA Modules:
  0.0 18.4 jit_solution(9690882653824450558)
XLA Ops:
  0.6 17.1 %shard_map.59 = f32[2,16,8,128]{3,2,1,0:T(8,128)S(1)} custom-call(f32[16,8,128]{2,1,0:T(8,128)} %bitcast.3, f32[16,8,128]{2,1,0:T(8,128)} %bitcast.4, f32[16,8,128]{2,1,0:T(8,128)} %bitcast.5, f32[16,8,128]{2,1,0:T(8,128)} %q_in.1), custom_call_target="tpu_custom_call" | custom-call | tf_op jit(solution)/shard_map/pallas_call | solution.py:582
  17.8 0.7 %fusion = (f32[1,16,8,128]{3,2,1,0:T(8,128)}, f32[1,16,8,128]{3,2,1,0:T(8,128)}) fusion(f32[2,16,8,128]{3,2,1,0:T(8,128)S(1)} %shard_map.59), kind=kLoop, calls=%fused_computation | loop fusion | bytes 262144 | tf_op jit(solution)/shard_map/slice | solution.py:613

commit v8 on v7

--- a/solution.py
+++ b/solution.py
@@ -304,22 +304,26 @@
 
     nb = depth // BLOCK
 
-    def field(i, high):
-        at_row, at_right = row[:high], right[:high]
-        inside = (
+    def inside(i, high):
+        at_row = row[:high]
+        return (
             (at_row < rows)
             | ((at_row < rows + reach[i]) & (gx + 1 < nx))
             | ((at_row >= wide - reach[i]) & (gx > 0))
         )
-        inside_right = at_right & inside & (gy + 1 < ny)
-        inside_left = jnp.logical_not(at_right) & inside & (gy > 0)
-        blocks = [main_ref[i, n * BLOCK : (n + 1) * BLOCK, 0:high] for n in range(nb)]
-        if high > rows:
-            blocks = [jnp.where(inside[None], b, 0.0) for b in blocks]
-        side = jnp.where(
+
+    def side_field(i, high):
+        here, at_right = inside(i, high), right[:high]
+        inside_right = at_right & here & (gy + 1 < ny)
+        inside_left = jnp.logical_not(at_right) & here & (gy > 0)
+        return jnp.where(
             inside_right, side_ref[1, i, 0:high], jnp.where(inside_left, side_ref[0, i, 0:high], 0.0)
         )
-        return Field(blocks, side)
+
+    def field(i):
+        here = inside(i, wide)[None]
+        blocks = [jnp.where(here, main_ref[i, n * BLOCK : (n + 1) * BLOCK], 0.0) for n in range(nb)]
+        return Field(blocks, side_field(i, wide))
 
     def own(f):
         return jnp.concatenate([b[:, :rows] for b in f.blocks], axis=0)
@@ -395,15 +399,55 @@
             jnp.concatenate([f.side, g.side], axis=0),
         )
 
+    each = range(nb)
+    k, s, x0, q = (Field([main_ref[i, n * BLOCK : (n + 1) * BLOCK, 0:rows] for n in each], None) for i in range(4))
+    own_mob = Field([mobility(b) for b in s.blocks], None)
+
+    def face_at(nxt, scaling, i):
+        return coefficient(scaling)(k.at(i), nxt(k, i), own_mob.at(i), nxt(own_mob, i))
+
+    z_coef = Field([face_at(z_next, VERTICAL, i) for i in each], None)
+    z_before = Field([z_prev(z_coef, i) for i in each], None)
+    x_coef = Field([face_at(x_next, 1.0, i) for i in each], None)
+    x_before = Field([x_prev(x_coef, i) for i in each], None)
+
+    def z_around(i):
+        return z_coef.at(i) * z_next(x0, i) + z_before.at(i) * z_prev(x0, i)
+
+    def z_diag(i):
+        return STORAGE + z_coef.at(i) + z_before.at(i)
+
+    z_part = Field([z_around(i) for i in each], None)
+    x_part = Field([x_around(x0, x_coef, x_before, i) for i in each], None)
+    own_diag = Field([z_diag(i) for i in each], None)
+
     arrive_y(y_moves[:2])
-    k, s = field(0, rows), field(1, rows)
-    own_mob, own_coefs, own_before = zy_faces(k, s)
-    own_diag = zy_diag(own_coefs, own_before)
-    x_coef, x_before = x_faces(k, own_mob)
+    for i, f in enumerate((k, s, x0, q)):
+        f.side = side_field(i, rows)
+    own_mob.side = mobility(s.side)
+    z_coef.side = face_at(z_next, VERTICAL, None)
+    z_before.side = z_prev(z_coef, None)
+    x_coef.side = face_at(x_next, 1.0, None)
+    x_before.side = x_prev(x_coef, None)
+    z_part.side = z_around(None)
+    x_part.side = x_around(x0, x_coef, x_before, None)
+    own_diag.side = z_diag(None)
+    (y_coef,) = build(lambda i: [face_at(y_next, 1.0, i)], nb)
+    (y_before,) = build(lambda i: [y_prev(y_coef, i)], nb)
+    (own_diag,) = build(lambda i: [own_diag.at(i) + y_coef.at(i) + y_before.at(i)], nb)
     diag, inverse = whole_diag(own_diag, x_coef, x_before)
-    x0 = field(2, rows)
-    own_around = zy_around(x0, own_coefs, own_before)
-    u0 = start_field(x0, field(3, rows), own_around, x_coef, x_before, diag, inverse)
+    ahead, back = y_both(x0)
+    (own_around,) = build(
+        lambda i: [z_part.at(i) + y_coef.at(i) * ahead.at(i) + y_before.at(i) * back.at(i)], nb
+    )
+    own_coefs, own_before = (z_coef, y_coef), (z_before, y_before)
+    (u0,) = build(
+        lambda i: [
+            (q.at(i) + STORAGE * x0.at(i) - (diag.at(i) * x0.at(i) - (own_around.at(i) + x_part.at(i))))
+            * inverse.at(i)
+        ],
+        nb,
+    )
     for i, b in enumerate(u0.blocks):
         early_send[i * BLOCK : (i + 1) * BLOCK] = b
     early_send[depth] = u0.side
@@ -424,7 +468,7 @@
 
     arrive_y(y_moves[2:])
     arrive_x(0)
-    k, s = field(0, wide), field(1, wide)
+    k, s = field(0), field(1)
     halo_mob, halo_coefs, halo_before = zy_faces(lower(k), lower(s))
     halo_diag = zy_diag(halo_coefs, halo_before)
     x_coef, x_before = x_faces(k, join(own_mob, halo_mob))
@@ -433,7 +477,7 @@
     z_before, y_before = [join(f, g) for f, g in zip(own_before, halo_before)]
     coefs = (z_coef, x_coef, y_coef)
     arrive_x(1)
-    x0, q = field(2, wide), field(3, wide)
+    x0, q = field(2), field(3)
     partial = join(own_around, zy_around(lower(x0), halo_coefs, halo_before))
     u0 = start_field(x0, q, partial, x_coef, x_before, diag, inverse)
     for dx in (-1, 1):
@@ -505,6 +549,23 @@
             late_copy(dx).wait_recv()
 
     patch(u1, late_recv)
+    bases = [
+        build(lambda i: [c.at(i) * (v.at(i) - nxt(v, i)) for nxt, c in zip(NEXT, coefs)], nb) for v in (x0, u0, u1)
+    ]
+    for dx in (-1, 1):
+        @pl.when(has(dx, 0))
+        def _():
+            for copy in x_copies(dx):
+                copy.wait_send()
+            early_copy(dx).wait_send()
+            late_copy(dx).wait_send()
+
+    for dx, dy in y_moves:
+        @pl.when(has(dx, dy))
+        def _():
+            y_copy(dx, dy).wait_send()
+
+    share_copy(1, 1, count - 1).wait_send()
     share_copy(1, 1, count - 1).wait_recv()
     total = jnp.sum(slots[...], axis=0, keepdims=True)
     sums = jnp.sum(jnp.where(mine, total, 0.0), axis=1, keepdims=True)
@@ -517,11 +578,10 @@
     weight0 = step0 + step1 * (1.0 + conjugacy)
     weight1 = -step1 * step0
 
-    (pressure,) = build(lambda i: [x0.at(i) + weight0 * u0.at(i) + weight1 * u1.at(i)], nb)
     flows = [Field([], None) for _ in NEXT]
 
     def flux(i):
-        return [c.at(i) * (pressure.at(i) - nxt(pressure, i)) for nxt, c in zip(NEXT, coefs)]
+        return [x.at(i) + weight0 * a.at(i) + weight1 * b.at(i) for x, a, b in zip(*bases)]
 
     def water_at(i, frac, nexts):
         return [
@@ -538,7 +598,8 @@
     for w, value in zip(water, water_at(None, frac, [n.side for n in after])):
         w.side = value
     for i in range(nb):
-        out_ref[0, i * BLOCK : (i + 1) * BLOCK] = pressure.blocks[i][:, :rows]
+        pressure = x0.blocks[i] + weight0 * u0.blocks[i] + weight1 * u1.blocks[i]
+        out_ref[0, i * BLOCK : (i + 1) * BLOCK] = pressure[:, :rows]
         for f, value in zip(flows, flux(i)):
             f.blocks.append(value)
         for w, value in zip(water, water_at(i, frac, [n.blocks[i] for n in after])):
@@ -555,21 +616,6 @@
             w.blocks.append(value)
         second = moved(i, first.blocks[i], gained(i, frac.blocks[i]), water)
         out_ref[1, i * BLOCK : (i + 1) * BLOCK] = second[:, :rows]
-
-    for dx in (-1, 1):
-        @pl.when(has(dx, 0))
-        def _():
-            for copy in x_copies(dx):
-                copy.wait_send()
-            early_copy(dx).wait_send()
-            late_copy(dx).wait_send()
-
-    for dx, dy in y_moves:
-        @pl.when(has(dx, dy))
-        def _():
-            y_copy(dx, dy).wait_send()
-
-    share_copy(1, 1, count - 1).wait_send()
 
 
 def local(nx, ny, permeability, saturation, pressure_old, source):

time: 18.6 us -> 18.3 us (0.984)
  Pallas kernels: 17.1 us -> 16.9 us
    pallas_call x1, Pallas kernels: 17.1 us -> 16.9 us  [local(): pl.pallas_call(functools.partial(kernel, nx, ny), out_shape=jax.ShapeDtyp...]
where the time goes in v8:
time: 18.3 us; the launch traced here: 18.1 us
  Pallas kernels  16.9 us (92%)
  local copies, waits for them, and re-layouts  0.66 us (4%)
  between operations  0.64 us (3%)
    pallas_call x1, Pallas kernels, local(): pl.pallas_call(functools.partial(kernel, nx, ny), out_shape=jax.ShapeDtyp...  16.9 us
    slice x1, local copies, waits for them, and re-layouts, local(): return (outs[:1], outs[1:])  0.66 us

profile of v8, /device:TPU:0, one launch (start us, length us, event | category | flops | bytes accessed | tf_op | source)
XLA Modules:
  0.0 18.1 jit_solution(1407852740740084136)
XLA Ops:
  0.6 16.9 %shard_map.59 = f32[2,16,8,128]{3,2,1,0:T(8,128)S(1)} custom-call(f32[16,8,128]{2,1,0:T(8,128)} %bitcast.3, f32[16,8,128]{2,1,0:T(8,128)} %bitcast.4, f32[16,8,128]{2,1,0:T(8,128)} %bitcast.5, f32[16,8,128]{2,1,0:T(8,128)} %q_in.1), custom_call_target="tpu_custom_call" | custom-call | tf_op jit(solution)/shard_map/pallas_call | solution.py:628
  17.5 0.7 %fusion = (f32[1,16,8,128]{3,2,1,0:T(8,128)}, f32[1,16,8,128]{3,2,1,0:T(8,128)}) fusion(f32[2,16,8,128]{3,2,1,0:T(8,128)S(1)} %shard_map.59), kind=kLoop, calls=%fused_computation | loop fusion | bytes 262144 | tf_op jit(solution)/shard_map/slice | solution.py:659

commit v9 on v8

--- a/solution.py
+++ b/solution.py
@@ -218,14 +218,14 @@
         d = (dx + 1) // 2
         return [
             pltpu.make_async_remote_copy(
-                src_ref=ref.at[:, edge_rows(dx, reach[i])],
+                src_ref=main_ref.at[i, :, edge_rows(dx, reach[i])],
                 dst_ref=main_ref.at[i, :, halo_rows(dx, reach[i])],
                 send_sem=xsend.at[d * len(ins) + i],
                 recv_sem=xrecv.at[d * len(ins) + i],
                 device_id=at(dx, 0),
                 device_id_type=MESH,
             )
-            for i, ref in enumerate(ins)
+            for i in range(len(ins))
             if i // 2 in halves
         ]
 
@@ -268,12 +268,12 @@
         pack_ref[i] = packed(main_ref[i, :, 0:rows, :])
 
     pl.semaphore_wait(barrier, expected)
-    for dx, dy in y_moves:
-        @pl.when(has(dx, dy))
-        def _():
-            y_copy(dx, dy).start()
-
-    for half in range(2):
+    for half, moves in enumerate((y_moves[:2], y_moves[2:])):
+        for dx, dy in moves:
+            @pl.when(has(dx, dy))
+            def _():
+                y_copy(dx, dy).start()
+
         for dx in (-1, 1):
             @pl.when(has(dx, 0))
             def _():

time: 18.3 us -> 18.3 us (level)
  no operation moved by 1% of the time
where the time goes in v9:
time: 18.3 us; the launch traced here: 18.2 us
  Pallas kernels  16.9 us (92%)
  local copies, waits for them, and re-layouts  0.66 us (4%)
  between operations  0.64 us (3%)
    pallas_call x1, Pallas kernels, local(): pl.pallas_call(functools.partial(kernel, nx, ny), out_shape=jax.ShapeDtyp...  16.9 us
    slice x1, local copies, waits for them, and re-layouts, local(): return (outs[:1], outs[1:])  0.66 us

profile of v9, /device:TPU:0, one launch (start us, length us, event | category | flops | bytes accessed | tf_op | source)
XLA Modules:
  0.0 18.2 jit_solution(14136522453231698086)
XLA Ops:
  0.6 16.9 %shard_map.59 = f32[2,16,8,128]{3,2,1,0:T(8,128)S(1)} custom-call(f32[16,8,128]{2,1,0:T(8,128)} %bitcast.3, f32[16,8,128]{2,1,0:T(8,128)} %bitcast.4, f32[16,8,128]{2,1,0:T(8,128)} %bitcast.5, f32[16,8,128]{2,1,0:T(8,128)} %q_in.1), custom_call_target="tpu_custom_call" | custom-call | tf_op jit(solution)/shard_map/pallas_call | solution.py:628
  17.5 0.7 %fusion = (f32[1,16,8,128]{3,2,1,0:T(8,128)}, f32[1,16,8,128]{3,2,1,0:T(8,128)}) fusion(f32[2,16,8,128]{3,2,1,0:T(8,128)S(1)} %shard_map.59), kind=kLoop, calls=%fused_computation | loop fusion | bytes 262144 | tf_op jit(solution)/shard_map/slice | solution.py:659

commit v10 on v9

--- a/solution.py
+++ b/solution.py
@@ -8,7 +8,7 @@
 from jax.sharding import PartitionSpec as P
 
 HALO = 4
-BLOCK = 4
+BLOCK = 2
 STORAGE = 0.5
 VERTICAL = 0.1
 STEP = 0.05
@@ -570,11 +570,12 @@
     total = jnp.sum(slots[...], axis=0, keepdims=True)
     sums = jnp.sum(jnp.where(mine, total, 0.0), axis=1, keepdims=True)
     sa, sb, sc, sd = (sums[i : i + 1, :] for i in range(4))
-    step0 = sa / sb
+    over_a, over_b = 1.0 / sa, 1.0 / sb
+    step0 = sa * over_b
     next_energy = step0 * step0 * sc - sa
-    conjugacy = next_energy / sa
+    conjugacy = next_energy * over_a
     curvature = sb - 2.0 * step0 * sc + step0 * step0 * sd
-    step1 = next_energy / (curvature - conjugacy * next_energy / step0)
+    step1 = next_energy / (curvature - conjugacy * next_energy * sb * over_a)
     weight0 = step0 + step1 * (1.0 + conjugacy)
     weight1 = -step1 * step0
 

time: 18.3 us -> 18.3 us (level)
  no operation moved by 1% of the time
where the time goes in v10:
time: 18.3 us; the launch traced here: 18.2 us
  Pallas kernels  16.9 us (92%)
  local copies, waits for them, and re-layouts  0.66 us (4%)
  between operations  0.64 us (3%)
    pallas_call x1, Pallas kernels, local(): pl.pallas_call(functools.partial(kernel, nx, ny), out_shape=jax.ShapeDtyp...  16.9 us
    slice x1, local copies, waits for them, and re-layouts, local(): return (outs[:1], outs[1:])  0.66 us

profile of v10, /device:TPU:0, one launch (start us, length us, event | category | flops | bytes accessed | tf_op | source)
XLA Modules:
  0.0 18.2 jit_solution(14382964271202951906)
XLA Ops:
  0.6 16.9 %shard_map.59 = f32[2,16,8,128]{3,2,1,0:T(8,128)S(1)} custom-call(f32[16,8,128]{2,1,0:T(8,128)} %bitcast.3, f32[16,8,128]{2,1,0:T(8,128)} %bitcast.4, f32[16,8,128]{2,1,0:T(8,128)} %bitcast.5, f32[16,8,128]{2,1,0:T(8,128)} %q_in.1), custom_call_target="tpu_custom_call" | custom-call | tf_op jit(solution)/shard_map/pallas_call | solution.py:629
  17.5 0.7 %fusion = (f32[1,16,8,128]{3,2,1,0:T(8,128)}, f32[1,16,8,128]{3,2,1,0:T(8,128)}) fusion(f32[2,16,8,128]{3,2,1,0:T(8,128)S(1)} %shard_map.59), kind=kLoop, calls=%fused_computation | loop fusion | bytes 262144 | tf_op jit(solution)/shard_map/slice | solution.py:660

commit v11 on v10

--- a/solution.py
+++ b/solution.py
@@ -216,17 +216,18 @@
 
     def x_copies(dx, halves=(0, 1)):
         d = (dx + 1) // 2
+        groups = (pl.ds(0, 2), None, pl.ds(2, 1), pl.ds(3, 1))
         return [
             pltpu.make_async_remote_copy(
-                src_ref=main_ref.at[i, :, edge_rows(dx, reach[i])],
-                dst_ref=main_ref.at[i, :, halo_rows(dx, reach[i])],
+                src_ref=main_ref.at[groups[i], :, edge_rows(dx, reach[i])],
+                dst_ref=main_ref.at[groups[i], :, halo_rows(dx, reach[i])],
                 send_sem=xsend.at[d * len(ins) + i],
                 recv_sem=xrecv.at[d * len(ins) + i],
                 device_id=at(dx, 0),
                 device_id_type=MESH,
             )
             for i in range(len(ins))
-            if i // 2 in halves
+            if i // 2 in halves and groups[i] is not None
         ]
 
     def y_copy(dx, dy):

time: 18.3 us -> 18.3 us (level)
  no operation moved by 1% of the time
where the time goes in v11:
time: 18.3 us; the launch traced here: 18.2 us
  Pallas kernels  16.9 us (92%)
  local copies, waits for them, and re-layouts  0.66 us (4%)
  between operations  0.64 us (3%)
    pallas_call x1, Pallas kernels, local(): pl.pallas_call(functools.partial(kernel, nx, ny), out_shape=jax.ShapeDtyp...  16.9 us
    slice x1, local copies, waits for them, and re-layouts, local(): return (outs[:1], outs[1:])  0.66 us

profile of v11, /device:TPU:0, one launch (start us, length us, event | category | flops | bytes accessed | tf_op | source)
XLA Modules:
  0.0 18.2 jit_solution(5893133402025922760)
XLA Ops:
  0.6 16.9 %shard_map.59 = f32[2,16,8,128]{3,2,1,0:T(8,128)S(1)} custom-call(f32[16,8,128]{2,1,0:T(8,128)} %bitcast.3, f32[16,8,128]{2,1,0:T(8,128)} %bitcast.4, f32[16,8,128]{2,1,0:T(8,128)} %bitcast.5, f32[16,8,128]{2,1,0:T(8,128)} %q_in.1), custom_call_target="tpu_custom_call" | custom-call | tf_op jit(solution)/shard_map/pallas_call | solution.py:630
  17.5 0.7 %fusion = (f32[1,16,8,128]{3,2,1,0:T(8,128)}, f32[1,16,8,128]{3,2,1,0:T(8,128)}) fusion(f32[2,16,8,128]{3,2,1,0:T(8,128)S(1)} %shard_map.59), kind=kLoop, calls=%fused_computation | loop fusion | bytes 262144 | tf_op jit(solution)/shard_map/slice | solution.py:661
